TPU v7x, 32 devices: a whole 2x2x4 slice. The times are simulated.
32 devices in a mesh: groups: 2 (over y), dp: 4 (over x, core), tensor: 4 (over z).
Axes of the slice: x: 2, y: 2, z: 4, core: 2. Of those that a mesh axis runs over, the one named last changes fastest.
Arguments:
- tokens: bfloat16 [4096, 4096], P(('groups', 'dp')), parts along dimension 0, may hold values from -6 to 6
- weight: bfloat16 [4096, 14336], P(None, 'tensor'), may hold values from -0.09375 to 0.09375
- grad_act: bfloat16 [4096, 14336], P(('groups', 'dp'), 'tensor'), parts along dimension 0, may hold values from -6 to 6
- proj_in: bfloat16 [4096, 64], P('tensor'), may hold values from -0.09375 to 0.09375
- proj_out: bfloat16 [14336, 64], P('tensor'), may hold values from -0.046875 to 0.046875
- query_bank: float32 [128, 4096], P(('groups', 'dp')), parts along dimension 0, may hold values from -6 to 6
- query_index: int32 [256], P('groups'), parts along dimension 0, may hold values from 0 to 63, as said below
Outputs:
- grad_in_t: bfloat16 [4096, 4096], P('tensor', ('groups', 'dp')), parts along dimension 1
- gram: float32 [8192, 4096], P(('groups', 'dp', 'tensor')), parts along dimension 0
- scores: float32 [16, 128], P(('groups', 'dp')), parts along dimension 0
There are 2 independent parts, one for each index of `groups`. A program takes and returns all parts, laid end to end along the dimension named above; an argument that names none is the same for every part. Nothing has to cross between parts.
Inputs may be any that keep to these rules, and one draw needn't show every extreme that they name: `query_index`: rows of query_bank to score, repeats allowed.
All inputs are finite; a program needn't handle non-finite values.
Results may differ from a plain program's by a relative error of at most 0.005.
Values sent between devices are 32-bit elements; how exact they have to be, the bound alone decides.
No kernel may reach another device: no remote copies, remote signals or barrier semaphores. Data moves between devices by JAX's collectives and lax.ppermute only.
A program may use at most 192 MiB of HBM per device.

v0:
```python
import math

import jax
import jax.numpy as jnp
from jax import lax
from jax.sharding import PartitionSpec as P

K_IN = 64
K_OUT = 64
LEN = 256
DOCS_DEV = 2
SK = 4096


def body(tokens, weight, grad_act, proj_in, proj_out, query_bank, query_index):
    tensor_count = lax.axis_size("tensor")
    dp_count = lax.axis_size("dp")
    tensor_pos = lax.axis_index("tensor")
    preact = jnp.dot(tokens, weight, preferred_element_type=jnp.float32)
    sigmoid_pre = jax.nn.sigmoid(preact)
    slopes = sigmoid_pre * (1.0 + preact * (1.0 - sigmoid_pre))
    grad_pre = (grad_act.astype(jnp.float32) * slopes).astype(jnp.bfloat16)
    feat_width = proj_in.shape[0]
    tok_cols = lax.dynamic_slice_in_dim(tokens, tensor_pos * feat_width, feat_width, 1)
    part_in = jnp.dot(tok_cols, proj_in, preferred_element_type=jnp.float32)
    part_out = jnp.dot(grad_pre, proj_out, preferred_element_type=jnp.float32)
    factors = lax.psum(jnp.concatenate([part_in, part_out], axis=1), "tensor")
    factor_in = factors[:, :K_IN].reshape(DOCS_DEV, LEN, K_IN)
    factor_out = factors[:, K_IN:].reshape(DOCS_DEV, LEN, K_OUT)
    sketches = jnp.einsum("dti,dtj->dij", factor_out, factor_in, precision=lax.Precision.HIGHEST)
    sketches = sketches.reshape(DOCS_DEV, SK) / math.sqrt(LEN)
    grad_in_t = lax.psum_scatter(
        lax.dot_general(
            weight, grad_pre, (((1,), (1,)), ((), ())), preferred_element_type=jnp.float32
        ),
        "tensor",
        scatter_dimension=0,
        tiled=True,
    ).astype(jnp.bfloat16)
    gram_rows = SK // (dp_count * tensor_count)
    dp_span = SK // dp_count
    offsets = jnp.arange(gram_rows * lax.axis_size("dp"), dtype=jnp.int32)
    columns = offsets // gram_rows * dp_span + tensor_pos * gram_rows + offsets % gram_rows
    picked = jnp.take(sketches, columns, axis=1)
    gram = lax.psum_scatter(
        jnp.dot(picked.T, sketches, precision=lax.Precision.HIGHEST),
        "dp",
        scatter_dimension=0,
        tiled=True,
    )
    queries = lax.all_gather(query_bank, "dp", axis=0, tiled=True)
    chosen = jnp.take(queries, query_index, axis=0)
    scores = jnp.dot(sketches, chosen.T, precision=lax.Precision.HIGHEST) / math.sqrt(SK)
    return (grad_in_t, gram, scores)


def solution(mesh):
    in_specs = (
        P(("groups", "dp"), None),
        P(None, "tensor"),
        P(("groups", "dp"), "tensor"),
        P("tensor", None),
        P("tensor", None),
        P(("groups", "dp"), None),
        P("groups"),
    )
    out_specs = (
        P("tensor", ("groups", "dp")),
        P(("groups", "dp", "tensor"), None),
        P(("groups", "dp"), None),
    )
    return jax.shard_map(body, mesh=mesh, in_specs=in_specs, out_specs=out_specs, check_vma=False)
```

profile of v0, /device:TPU:16, one launch (start us, length us, event | category | flops | bytes accessed | tf_op | source)
XLA Modules:
  0.0 360.0 jit_solution(13725874031268702022)
XLA Ops:
  8.0 0.0 copy-start
  8.0 0.0 all-reduce.2.cloned.1.call-start
  8.1 0.0 copy-start.2
  8.1 0.0 copy-start.3
  8.1 23.8 %fusion.41 = f32[512,3584]{1,0:T(8,128)} fusion(bf16[512,4096]{1,0:T(8,128)(2,1)} %param.7, bf16[4096,3584]{1,0:T(8,128)(2,1)} %param.8), kind=kOutput, calls=%fused_computation.60 | convolution fusion | flops 15032385536 | bytes 40894464 | tf_op jit(solution)/shard_map/dot_general | solution.py:19
  31.9 0.0 copy-done.2
  31.9 1.7 fusion.11
  33.6 0.0 copy-done
  33.6 0.0 copy-done.3
  33.6 5.1 %fusion = f32[512,64]{0,1:T(8,128)S(1)} fusion(bf16[3584,64]{0,1:T(8,128)(2,1)S(1)} %copy-done, f32[512,3584]{1,0:T(8,128)} %fusion.41, bf16[512,3584]{1,0:T(8,128)(2,1)S(1)} %copy-done.3), kind=kOutput, calls=%fused_computation.3 | convolution fusion | flops 253231104 | bytes 11599872 | tf_op jit(solution)/shard_map/dot_general | solution.py:26
  38.7 0.7 pad_maximum_fusion
  39.4 0.0 all-reduce.2.cloned.1.call-update
  39.5 0.0 all-gather.2.cloned.1.call-start
  39.5 0.5 all-gather.2.cloned.1.call-update
  40.0 0.0 reduce-scatter.3.cloned.1.call-start
  40.1 27.3 %fusion.2 = f32[4096,512]{0,1:T(8,128)} fusion(bf16[4096,3584]{1,0:T(8,128)(2,1)} %param.8, f32[512,3584]{1,0:T(8,128)} %fusion.41, bf16[512,3584]{1,0:T(8,128)(2,1)} %param.9), kind=kOutput, calls=%fused_computation.5 | convolution fusion | flops 15050735616 | bytes 48758784 | tf_op jit(solution)/shard_map/dot_general | solution.py:33
  67.4 0.0 reduce-scatter.3.cloned.1.call-update
  67.5 0.2 reduce-scatter.5.cloned.1.call-start
  67.7 8.0 %all-reduce.2.cloned.1.call-done = f32[512,128]{0,1:T(8,128)} async-done(((f32[512,128]{0,1:T(8,128)}), f32[512,128]{0,1:T(8,128)}) %all-reduce.2.cloned.1.call-update) | async-done | bytes 262160 | tf_op jit(solution)/shard_map/psum | solution.py:27
  75.8 1.0 fusion.40
  76.8 0.3 convolution_multiply_fusion
  77.0 0.1 div.34
  77.1 0.6 copy.16
  77.8 2.8 gather_fusion
  80.6 16.4 %fusion.14 = f32[1024,4096]{1,0:T(8,128)} fusion(f32[2,4096]{1,0:T(2,128)S(1)} %div.34, f32[1024,2]{1,0:T(8,128)S(1)} %gather_fusion, pred[1024]{0:T(1024)(128)(4,1)S(1)} %compare_and_fusion), kind=kOutput, calls=%fused_computation.16 | convolution fusion | flops 100665344 | bytes 16819200 | tf_op jit(solution)/shard_map/dot_general | solution.py:46
  97.0 0.0 copy-start.4
  97.0 0.0 reduce-scatter.5.cloned.1.call-update
  97.0 0.6 copy-done.4
  97.7 0.0 all-gather.2.cloned.1.call-done
  97.7 0.0 copy-start.1
  97.7 3.5 gather_fusion.1
  101.2 2.4 fusion.7
  103.6 119.8 %reduce-scatter.3.cloned.1.call-done = f32[1024,512]{0,1:T(8,128)} async-done(((f32[4096,512]{0,1:T(8,128)}), f32[1024,512]{0,1:T(8,128)}) %reduce-scatter.3.cloned.1.call-update) | async-done | bytes 2097168 | tf_op jit(solution)/shard_map/reduce_scatter | solution.py:32
  223.4 1.7 convert_element_type.11
  225.2 1.3 copy.17
  226.5 126.4 %reduce-scatter.5.cloned.1.call-done = f32[256,4096]{1,0:T(8,128)} async-done(((f32[1024,4096]{1,0:T(8,128)}), f32[256,4096]{1,0:T(8,128)}) %reduce-scatter.5.cloned.1.call-update) | async-done | bytes 4194320 | tf_op jit(solution)/shard_map/reduce_scatter | solution.py:45
  352.9 0.0 copy-done.1
  (6 shorter events, 0.1 us)
Async XLA Ops:
  8.0 25.6 %copy-start = (bf16[3584,64]{0,1:T(8,128)(2,1)S(1)}, bf16[3584,64]{0,1:T(8,128)(2,1)}, u32[]{:S(2)}) copy-start(bf16[3584,64]{0,1:T(8,128)(2,1)} %param.11) | copy-start | bytes 1376260
  8.0 67.8 %all-reduce.2.cloned.1.call-start = ((), (), s32[]{:S(2)}) async-start(), calls=%async_computation.3 | async-start | bytes 524288 | tf_op jit(solution)/shard_map/psum | solution.py:27
  8.1 23.9 %copy-start.2 = (bf16[1024,64]{0,1:T(8,128)(2,1)S(1)}, bf16[1024,64]{0,1:T(8,128)(2,1)}, u32[]{:S(2)}) copy-start(bf16[1024,64]{0,1:T(8,128)(2,1)} %param.10) | copy-start | bytes 393220
  8.1 25.5 %copy-start.3 = (bf16[512,3584]{1,0:T(8,128)(2,1)S(1)}, bf16[512,3584]{1,0:T(8,128)(2,1)}, u32[]{:S(2)}) copy-start(bf16[512,3584]{1,0:T(8,128)(2,1)} %param.9) | copy-start | bytes 11010052
  39.5 58.2 %all-gather.2.cloned.1.call-start = ((), (), s32[]{:S(2)}) async-start(), calls=%async_computation.5 | async-start | bytes 1310720 | tf_op jit(solution)/shard_map/all_gather | solution.py:51
  40.0 183.4 %reduce-scatter.3.cloned.1.call-start = ((), (), s32[]{:S(2)}) async-start(), calls=%async_computation.2 | async-start | bytes 10485760 | tf_op jit(solution)/shard_map/reduce_scatter | solution.py:32
  67.5 285.4 %reduce-scatter.5.cloned.1.call-start = ((), (), s32[]{:S(2)}) async-start(), calls=%async_computation.4 | async-start | bytes 20971520 | tf_op jit(solution)/shard_map/reduce_scatter | solution.py:45
  97.0 0.7 copy-start.4
  97.7 255.2 %copy-start.1 = (bf16[3584,64]{0,1:T(8,128)(2,1)S(1)}, bf16[3584,64]{0,1:T(8,128)(2,1)}, u32[]{:S(2)}) copy-start(bf16[3584,64]{0,1:T(8,128)(2,1)} %param.11) | copy-start | bytes 1376260
Sparse Core Ops, SparseCore 0:
  39.6 36.1 all-reduce.1
  78.2 145.1 reduce-scatter.2
  226.8 126.0 reduce-scatter.4
Sparse Core Ops, SparseCore 1:
  41.5 17.6 all-gather.1
where the time goes:
time: 362 us; the launch traced here: 360 us
  waiting for transfers between devices  255 us (70%)
  matrix products  77 us (21%)
  between operations  15.3 us (4%)
  local copies, waits for them, and re-layouts  10 us (3%)
    reduce_scatter x1, waiting for transfers between devices, body(): lax.psum_scatter(jnp.dot(picked.T, sketches, precision=lax.Precision.HIGH...  126 us
    reduce_scatter x1, waiting for transfers between devices, body(): lax.psum_scatter(lax.dot_general(weight, grad_pre, (((1,), (1,)), ((), ()...  120 us
    dot_general x1, matrix products, body(): lax.dot_general(weight, grad_pre, (((1,), (1,)), ((), ())), preferred_ele...  27.3 us
    dot_general x1, matrix products, body(): preact = jnp.dot(tokens, weight, preferred_element_type=jnp.float32)  23.8 us
    dot_general x1, matrix products, body(): jnp.dot(picked.T, sketches, precision=lax.Precision.HIGHEST)  16.4 us
    psum x1, waiting for transfers between devices, body(): factors = lax.psum(jnp.concatenate([part_in, part_out], axis=1), 'tensor')  8.03 us
  transfers between devices with their start and end apart: 4, of which 3 were waited for; matrix products, arithmetic and copies ran while one was open for 16% of the time, Pallas kernels for 0%

commit v1 on v0

v1 whole, which is shorter than its diff:
```python
import math

import jax
import jax.numpy as jnp
from jax import lax
from jax.sharding import PartitionSpec as P

LEN = 256
SK = 4096
HIGH = lax.Precision.HIGHEST


def line_pairs(count, step, color):
    up = [(i, i + 1) for i in range(count - 1) if i < step and i % 2 == color]
    down = [(j, j - 1) for j in range(1, count) if count - 1 - j < step and (j - 1) % 2 == color]
    return up + down


def swap_sum(x, axis, count):
    hop = 1
    while hop < count:
        x = x + lax.ppermute(x, axis, [(i, i ^ hop) for i in range(count)])
        hop *= 2
    return x


def swap_gather(x, axis, count, pos, dim):
    hop = 1
    while hop < count:
        other = lax.ppermute(x, axis, [(i, i ^ hop) for i in range(count)])
        low = (pos // hop) % 2 == 0
        x = jnp.where(low, jnp.concatenate([x, other], dim), jnp.concatenate([other, x], dim))
        hop *= 2
    return x


def body(tokens, weight, grad_act, proj_in, proj_out, query_bank, query_index):
    n = lax.axis_size("tensor")
    m = lax.axis_size("dp")
    pos = lax.axis_index("tensor")
    dp_pos = lax.axis_index("dp")
    docs = tokens.shape[0] // LEN
    feat = proj_in.shape[0]
    sign = jnp.where(pos % 2 == 0, -1, 1)

    tok_cols = lax.dynamic_slice_in_dim(tokens, pos * feat, feat, 1)
    factor_in = swap_sum(jnp.dot(tok_cols, proj_in, preferred_element_type=jnp.float32), "tensor", n)

    halves = 2
    chunk = feat // halves
    grads = []
    for d in range(docs):
        rows = slice(d * LEN, (d + 1) * LEN)
        preact = jnp.dot(tokens[rows], weight, preferred_element_type=jnp.float32)
        sig = jax.nn.sigmoid(preact)
        slopes = sig * (1.0 + preact * (1.0 - sig))
        grads.append((grad_act[rows].astype(jnp.float32) * slopes).astype(jnp.bfloat16))

    def block(k, d, r):
        start = ((pos + sign * k) % n) * feat + r * chunk
        part = lax.dynamic_slice_in_dim(weight, start, chunk, 0)
        return lax.dot_general(part, grads[d], (((1,), (1,)), ((), ())), preferred_element_type=jnp.float32)

    outs = [[None] * halves for _ in range(docs)]
    cells = [(d, r) for d in range(docs) for r in range(halves)]
    blocks = {}
    for k in list(range(1, n)) + [0]:
        for d, r in cells:
            blocks[k, d, r] = block(k, d, r)
    even = {c: None for c in cells}
    odd = {c: None for c in cells}
    for step in range(1, n):
        for c in cells:
            send_even = blocks[(step, *c)]
            if odd[c] is not None:
                send_even = send_even + odd[c]
            new_even = lax.ppermute(send_even, "tensor", line_pairs(n, step, 0))
            new_odd = None
            if line_pairs(n, step, 1):
                send_odd = blocks[(n - step, *c)] + even[c]
                new_odd = lax.ppermute(send_odd, "tensor", line_pairs(n, step, 1))
            even[c], odd[c] = new_even, new_odd
    for d, r in cells:
        total = blocks[0, d, r] + even[d, r]
        if odd[d, r] is not None:
            total = total + odd[d, r]
        outs[d][r] = total.astype(jnp.bfloat16)
    grad_in_t = jnp.concatenate([jnp.concatenate(row, 0) for row in outs], 1)

    sketches = []
    for d in range(docs):
        part_out = jnp.dot(grads[d], proj_out, preferred_element_type=jnp.float32)
        sketches.append(
            lax.dot_general(part_out, factor_in[d * LEN:(d + 1) * LEN], (((0,), (0,)), ((), ())), precision=HIGH)
        )
    sketches = jnp.stack(sketches).reshape(docs, SK) / math.sqrt(LEN)
    sketches = swap_sum(sketches, "tensor", n)
    everyone = swap_gather(sketches, "dp", m, dp_pos, 0)
    gram_rows = SK // (m * n)
    mine = lax.dynamic_slice_in_dim(everyone, (dp_pos * n + pos) * gram_rows, gram_rows, 1)
    gram = lax.dot_general(mine, everyone, (((0,), (0,)), ((), ())), precision=HIGH)

    scores = lax.dot_general(everyone, query_bank, (((1,), (1,)), ((), ())), precision=HIGH) / math.sqrt(SK)
    scores = swap_gather(scores, "dp", m, dp_pos, 1)
    scores = lax.dynamic_slice_in_dim(scores, dp_pos * docs, docs, 0)
    places = jnp.arange(scores.shape[1], dtype=query_index.dtype)
    picked = jnp.where(query_index[None, :, None] == places[None, None, :], scores[:, None, :], 0.0)
    return (grad_in_t, gram, jnp.sum(picked, -1))


def solution(mesh):
    in_specs = (
        P(("groups", "dp"), None),
        P(None, "tensor"),
        P(("groups", "dp"), "tensor"),
        P("tensor", None),
        P("tensor", None),
        P(("groups", "dp"), None),
        P("groups"),
    )
    out_specs = (
        P("tensor", ("groups", "dp")),
        P(("groups", "dp", "tensor"), None),
        P(("groups", "dp"), None),
    )
    return jax.shard_map(body, mesh=mesh, in_specs=in_specs, out_specs=out_specs, check_vma=False)
```

time: 362 us -> 234 us (0.65)
  waiting for transfers between devices: 255 us -> 59.5 us
  starting transfers between devices: 0.35 us -> 47.2 us
  matrix products: 77 us -> 107 us
  between operations: 15.3 us -> 1.35 us
  other arithmetic: 2.52 us -> 15.3 us
  local copies, waits for them, and re-layouts: 10 us -> 0.91 us
    reduce_scatter x2 -> x0, waiting for transfers between devices: 246 us -> none  [the longest x1 126 us: body(): lax.psum_scatter(jnp.dot(picked.T, sketches, precision=lax.Precision.HIGH...]
    ppermute x0 -> x28, waiting for transfers between devices: none -> 59.5 us  [the longest x8 38.5 us: body(): new_odd = lax.ppermute(send_odd, 'tensor', line_pairs(n, step, 1))]
    ppermute x0 -> x28, starting transfers between devices: none -> 47.2 us  [the longest x8 25.1 us: body(): new_odd = lax.ppermute(send_odd, 'tensor', line_pairs(n, step, 1))]
    dot_general x7 -> x25, matrix products: 77 us -> 107 us  [the longest x16 66.7 us: block(): lax.dot_general(part, grads[d], (((1,), (1,)), ((), ())), preferred_eleme...]
    add x0 -> x12, other arithmetic: none -> 12.9 us  [the longest x4 6.82 us: body(): send_odd = blocks[n - step, *c] + even[c]]
    psum x1 -> x0, waiting for transfers between devices: 8.03 us -> none  [body(): factors = lax.psum(jnp.concatenate([part_in, part_out], axis=1), 'tensor')]
    gather x2 -> x0, local copies, waits for them, and re-layouts: 6.32 us -> none  [the longest x1 3.51 us: body(): chosen = jnp.take(queries, query_index, axis=0)]
  transfers between devices with their start and end apart: 4 -> 28, of which waited for: 3 -> 10; matrix products, arithmetic and copies ran while one was open for 16% -> 52% of each run, Pallas kernels for 0% -> 0%
where the time goes in v1:
time: 234 us; the launch traced here: 232 us
  matrix products  107 us (46%)
  waiting for transfers between devices  59.5 us (25%)
  starting transfers between devices  47.2 us (20%)
  other arithmetic  15.3 us (7%)
    dot_general x16, matrix products, block(): lax.dot_general(part, grads[d], (((1,), (1,)), ((), ())), preferred_eleme...  66.7 us
    ppermute x8, waiting for transfers between devices, body(): new_odd = lax.ppermute(send_odd, 'tensor', line_pairs(n, step, 1))  38.5 us
    dot_general x2, matrix products, body(): preact = jnp.dot(tokens[rows], weight, preferred_element_type=jnp.float32)  29.3 us
    ppermute x8, starting transfers between devices, body(): new_odd = lax.ppermute(send_odd, 'tensor', line_pairs(n, step, 1))  25.1 us
    ppermute x12, waiting for transfers between devices, body(): new_even = lax.ppermute(send_even, 'tensor', line_pairs(n, step, 0))  13.7 us
    ppermute x12, starting transfers between devices, body(): new_even = lax.ppermute(send_even, 'tensor', line_pairs(n, step, 0))  10.8 us
    ppermute x4, starting transfers between devices, swap_sum(): x = x + lax.ppermute(x, axis, [(i, i ^ hop) for i in range(count)])  9.12 us
    add x4, other arithmetic, body(): send_odd = blocks[n - step, *c] + even[c]  6.82 us
  transfers between devices with their start and end apart: 28, of which 10 were waited for; matrix products, arithmetic and copies ran while one was open for 52% of the time, Pallas kernels for 0%

profile of v1, /device:TPU:16, one launch (start us, length us, event | category | flops | bytes accessed | tf_op | source)
XLA Modules:
  0.0 231.8 jit_solution(16288424527515186866)
XLA Ops:
  0.7 1.7 fusion.40
  2.4 1.6 collective-permute-start.20
  4.0 14.9 %multiply_convert_fusion = bf16[256,3584]{1,0:T(8,128)(2,1)S(1)} fusion(bf16[4096,3584]{1,0:T(8,128)(2,1)} %param.8, bf16[512,4096]{1,0:T(8,128)(2,1)} %param.7, bf16[512,3584]{1,0:T(8,128)(2,1)} %param.9), kind=kOutput, calls=%fused_computation | convolution fusion | flops 7525367808 | bytes 35127296 | tf_op jit(solution)/shard_map/dot_general | solution.py:54
  18.9 4.7 %fusion.20 = f32[512,256]{1,0:T(8,128)} fusion(bf16[256,3584]{1,0:T(8,128)(2,1)S(1)} %multiply_convert_fusion, bf16[4096,3584]{1,0:T(8,128)(2,1)} %param.8, s32[]{:T(128)S(6)} %select_n.154), kind=kOutput, calls=%fused_computation.22 | convolution fusion | flops 939524096 | bytes 6029316 | tf_op jit(solution)/shard_map/dot_general | solution.py:62
  23.6 1.3 collective-permute-start.13
  24.9 4.1 %fusion.4 = f32[512,256]{1,0:T(8,128)} fusion(bf16[256,3584]{1,0:T(8,128)(2,1)S(1)} %multiply_convert_fusion, bf16[4096,3584]{1,0:T(8,128)(2,1)} %param.8, s32[]{:T(128)S(6)} %select_n.159), kind=kOutput, calls=%fused_computation.6 | convolution fusion | flops 939524096 | bytes 6029316 | tf_op jit(solution)/shard_map/dot_general | solution.py:62
  29.0 1.3 collective-permute-start.18
  30.3 14.5 %multiply_convert_fusion.1 = bf16[256,3584]{1,0:T(8,128)(2,1)S(1)} fusion(bf16[4096,3584]{1,0:T(8,128)(2,1)} %param.8, bf16[512,4096]{1,0:T(8,128)(2,1)S(1)} %copy-done.11, bf16[512,3584]{1,0:T(8,128)(2,1)} %param.9), kind=kOutput, calls=%fused_computation.1 | convolution fusion | flops 7525367808 | bytes 35127296 | tf_op jit(solution)/shard_map/dot_general | solution.py:54
  44.8 4.0 %fusion.22 = f32[512,256]{1,0:T(8,128)} fusion(bf16[256,3584]{1,0:T(8,128)(2,1)S(1)} %multiply_convert_fusion.1, bf16[4096,3584]{1,0:T(8,128)(2,1)} %param.8, s32[]{:T(128)S(6)} %select_n.154), kind=kOutput, calls=%fused_computation.24 | convolution fusion | flops 939524096 | bytes 6029316 | tf_op jit(solution)/shard_map/dot_general | solution.py:62
  48.7 1.3 collective-permute-start.3
  50.0 4.0 %fusion.6 = f32[512,256]{1,0:T(8,128)} fusion(bf16[256,3584]{1,0:T(8,128)(2,1)S(1)} %multiply_convert_fusion.1, bf16[4096,3584]{1,0:T(8,128)(2,1)} %param.8, s32[]{:T(128)S(6)} %select_n.159), kind=kOutput, calls=%fused_computation.8 | convolution fusion | flops 939524096 | bytes 6029316 | tf_op jit(solution)/shard_map/dot_general | solution.py:62
  54.0 1.5 collective-permute-start.8
  55.5 4.6 %fusion.8 = f32[512,256]{1,0:T(8,128)} fusion(bf16[256,3584]{1,0:T(8,128)(2,1)} %copy-done.1, bf16[4096,3584]{1,0:T(8,128)(2,1)} %param.8, s32[]{:T(128)S(6)} %select_n.158), kind=kOutput, calls=%fused_computation.10 | convolution fusion | flops 939524096 | bytes 6029316 | tf_op jit(solution)/shard_map/dot_general | solution.py:62
  60.1 4.0 %fusion.10 = f32[512,256]{1,0:T(8,128)} fusion(bf16[256,3584]{1,0:T(8,128)(2,1)S(1)} %multiply_convert_fusion.1, bf16[4096,3584]{1,0:T(8,128)(2,1)} %param.8, s32[]{:T(128)S(6)} %select_n.158), kind=kOutput, calls=%fused_computation.12 | convolution fusion | flops 939524096 | bytes 6029316 | tf_op jit(solution)/shard_map/dot_general | solution.py:62
  64.1 3.7 %fusion.12 = f32[512,256]{1,0:T(8,128)S(1)} fusion(bf16[256,3584]{1,0:T(8,128)(2,1)} %copy-done.1, bf16[4096,3584]{1,0:T(8,128)(2,1)} %param.8, s32[]{:T(128)S(6)} %select_n.157), kind=kOutput, calls=%fused_computation.14 | convolution fusion | flops 939524096 | bytes 6029316 | tf_op jit(solution)/shard_map/dot_general | solution.py:62
  67.8 3.2 %fusion.14 = f32[512,256]{1,0:T(8,128)S(1)} fusion(bf16[256,3584]{1,0:T(8,128)(2,1)S(1)} %multiply_convert_fusion.1, bf16[4096,3584]{1,0:T(8,128)(2,1)} %param.8, s32[]{:T(128)S(6)} %select_n.157), kind=kOutput, calls=%fused_computation.16 | convolution fusion | flops 939524096 | bytes 6029316 | tf_op jit(solution)/shard_map/dot_general | solution.py:62
  71.0 4.5 %fusion.24 = f32[512,256]{1,0:T(8,128)} fusion(bf16[256,3584]{1,0:T(8,128)(2,1)} %copy-done.1, bf16[4096,3584]{1,0:T(8,128)(2,1)} %param.8, s32[]{:T(128)S(6)} %select_n.152), kind=kOutput, calls=%fused_computation.26 | convolution fusion | flops 939524096 | bytes 6029316 | tf_op jit(solution)/shard_map/dot_general | solution.py:62
  75.6 4.1 %fusion.26 = f32[512,256]{1,0:T(8,128)} fusion(bf16[256,3584]{1,0:T(8,128)(2,1)S(1)} %multiply_convert_fusion.1, bf16[4096,3584]{1,0:T(8,128)(2,1)} %param.8, s32[]{:T(128)S(6)} %select_n.152), kind=kOutput, calls=%fused_computation.28 | convolution fusion | flops 939524096 | bytes 6029316 | tf_op jit(solution)/shard_map/dot_general | solution.py:62
  79.7 1.3 fusion.72
  81.0 1.6 add.255
  82.6 4.0 %collective-permute-start.21 = (f32[512,64]{0,1:T(8,128)}, f32[512,64]{0,1:T(8,128)}, u32[]{:S(2)}, u32[]{:S(2)}) collective-permute-start(f32[512,64]{0,1:T(8,128)} %add.255), channel_id=1, source_target_pairs={{0,2},{1,3},{2,0},{3,1},{4,6},{5,7},{6,4},{7,5},{8,10},{9,11},{10,... | collective-permute-start | bytes 393224 | tf_op jit(solution)/shard_map/ppermute | solution.py:22
  87.2 5.0 %collective-permute-done.21 = f32[512,64]{0,1:T(8,128)} collective-permute-done((f32[512,64]{0,1:T(8,128)}, f32[512,64]{0,1:T(8,128)}, u32[]{:S(2)}, u32[]{:S(2)}) %collective-permute-start.21) | collective-permute-done | bytes 131104 | tf_op jit(solution)/shard_map/ppermute | solution.py:22
  92.1 1.0 add.256
  93.8 1.3 fusion.42
  95.2 1.2 fusion.44
  96.5 2.3 collective-permute-start.22
  98.8 4.6 %fusion.28 = f32[512,256]{1,0:T(8,128)} fusion(bf16[256,3584]{1,0:T(8,128)(2,1)} %copy-done.1, bf16[4096,3584]{1,0:T(8,128)(2,1)} %param.8, s32[]{:T(128)S(6)} %select_n.148), kind=kOutput, calls=%fused_computation.30 | convolution fusion | flops 939524096 | bytes 6029316 | tf_op jit(solution)/shard_map/dot_general | solution.py:62
  103.4 1.2 collective-permute-start.23
  104.7 4.0 %fusion.30 = f32[512,256]{1,0:T(8,128)} fusion(bf16[256,3584]{1,0:T(8,128)(2,1)S(1)} %multiply_convert_fusion.1, bf16[4096,3584]{1,0:T(8,128)(2,1)} %param.8, s32[]{:T(128)S(6)} %select_n.148), kind=kOutput, calls=%fused_computation.32 | convolution fusion | flops 939524096 | bytes 6029316 | tf_op jit(solution)/shard_map/dot_general | solution.py:62
  108.9 1.1 collective-permute-done.24
  110.0 1.7 collective-permute-start.25
  111.7 4.6 %fusion.68 = (f32[512,256]{1,0:T(8,128)}, f32[512,256]{1,0:T(8,128)S(1)}) fusion(f32[512,256]{1,0:T(8,128)} %collective-permute-done.13, bf16[256,3584]{1,0:T(8,128)(2,1)} %copy-done.1, bf16[4096,3584]{1,0:T(8,128)(2,1)} %param.8, s32[]{:T(128)S(6)} %select_n.156), kind=kOutput, calls=%fused_computation.80 | convolution fusion | flops 939655168 | bytes 7077892 | tf_op jit(solution)/shard_map/dot_general | solution.py:62
  116.4 1.3 collective-permute-start.10
  117.7 4.1 %fusion.67 = (f32[512,256]{1,0:T(8,128)}, f32[512,256]{1,0:T(8,128)S(1)}) fusion(f32[512,256]{1,0:T(8,128)} %collective-permute-done.18, bf16[256,3584]{1,0:T(8,128)(2,1)S(1)} %copy-done.3, bf16[4096,3584]{1,0:T(8,128)(2,1)} %param.8, s32[]{:T(128)S(6)} %select_n.160), kind=kOutput, calls=%fused_computation.79 | convolution fusion | flops 939655168 | bytes 7077892 | tf_op jit(solution)/shard_map/dot_general | solution.py:62
  121.8 1.3 collective-permute-start.15
  123.1 4.1 %fusion.70 = (f32[512,256]{1,0:T(8,128)}, f32[512,256]{1,0:T(8,128)S(1)}) fusion(f32[512,256]{1,0:T(8,128)} %collective-permute-done.3, bf16[256,3584]{1,0:T(8,128)(2,1)S(1)} %multiply_convert_fusion.1, bf16[4096,3584]{1,0:T(8,128)(2,1)} %param.8, s32[]{:T(128)S(6)} %select_n.156), kind=kOutput, calls=%fused_computation.82 | convolution fusion | flops 939655168 | bytes 7077892 | tf_op jit(solution)/shard_map/dot_general | solution.py:62
  127.2 1.3 collective-permute-start
  128.5 4.3 %fusion.69 = (f32[512,256]{1,0:T(8,128)}, f32[512,256]{1,0:T(8,128)}) fusion(f32[512,256]{1,0:T(8,128)} %collective-permute-done.8, bf16[256,3584]{1,0:T(8,128)(2,1)S(1)} %multiply_convert_fusion.1, bf16[4096,3584]{1,0:T(8,128)(2,1)} %param.8, s32[]{:T(128)S(6)} %select_n.160), kind=kOutput, calls=%fused_computation.81 | convolution fusion | flops 939655168 | bytes 7077892 | tf_op jit(solution)/shard_map/dot_general | solution.py:62
  132.8 1.4 collective-permute-start.5
  134.2 1.9 add.242
  136.1 3.3 %collective-permute-start.11 = (f32[512,256]{1,0:T(8,128)}, f32[512,256]{1,0:T(8,128)}, u32[]{:S(2)}, u32[]{:S(2)}) collective-permute-start(f32[512,256]{1,0:T(8,128)} %add.242), channel_id=1, source_target_pairs={{1,2},{2,1},{5,6},{6,5},{9,10},{10,9},{13,14},{14,13},{17,18},{18,... | collective-permute-start | bytes 1572872 | tf_op jit(solution)/shard_map/ppermute | solution.py:81
  139.4 4.9 %collective-permute-done.15 = f32[512,256]{1,0:T(8,128)S(1)} collective-permute-done((f32[512,256]{1,0:T(8,128)S(1)}, f32[512,256]{1,0:T(8,128)S(1)}, u32[]{:S(2)}, u32[]{:S(2)}) %collective-permute-start.15) | collective-permute-done | bytes 524320 | tf_op jit(solution)/shard_map/ppermute | solution.py:77
  144.3 1.9 add.247
  146.2 3.3 %collective-permute-start.16 = (f32[512,256]{1,0:T(8,128)}, f32[512,256]{1,0:T(8,128)}, u32[]{:S(2)}, u32[]{:S(2)}) collective-permute-start(f32[512,256]{1,0:T(8,128)} %add.247), channel_id=1, source_target_pairs={{1,2},{2,1},{5,6},{6,5},{9,10},{10,9},{13,14},{14,13},{17,18},{18,... | collective-permute-start | bytes 1572872 | tf_op jit(solution)/shard_map/ppermute | solution.py:81
  149.5 6.0 %collective-permute-done = f32[512,256]{1,0:T(8,128)S(1)} collective-permute-done((f32[512,256]{1,0:T(8,128)S(1)}, f32[512,256]{1,0:T(8,128)S(1)}, u32[]{:S(2)}, u32[]{:S(2)}) %collective-permute-start) | collective-permute-done | bytes 524320 | tf_op jit(solution)/shard_map/ppermute | solution.py:77
  155.5 1.9 add.222
  157.4 3.3 %collective-permute-start.1 = (f32[512,256]{1,0:T(8,128)}, f32[512,256]{1,0:T(8,128)}, u32[]{:S(2)}, u32[]{:S(2)}) collective-permute-start(f32[512,256]{1,0:T(8,128)} %add.222), channel_id=1, source_target_pairs={{1,2},{2,1},{5,6},{6,5},{9,10},{10,9},{13,14},{14,13},{17,18},{18,... | collective-permute-start | bytes 1572872 | tf_op jit(solution)/shard_map/ppermute | solution.py:81
  161.1 1.2 collective-permute-done.26
  162.8 2.8 %collective-permute-done.5 = f32[512,256]{1,0:T(8,128)S(1)} collective-permute-done((f32[512,256]{1,0:T(8,128)}, f32[512,256]{1,0:T(8,128)S(1)}, u32[]{:S(2)}, u32[]{:S(2)}) %collective-permute-start.5) | collective-permute-done | bytes 524320 | tf_op jit(solution)/shard_map/ppermute | solution.py:77
  165.7 3.4 %collective-permute-start.14 = (f32[512,256]{1,0:T(8,128)}, f32[512,256]{1,0:T(8,128)S(1)}, u32[]{:S(2)}, u32[]{:S(2)}) collective-permute-start(f32[512,256]{1,0:T(8,128)} %get-tuple-element.5), channel_id=1, source_target_pairs={{1,2},{2,1},{5,6},{6,5},{9,10},{10,9},{13,14},{14,13},{17,18},{18,... | collective-permute-start | bytes 1572872 | tf_op jit(solution)/shard_map/ppermute | solution.py:81
  169.1 1.1 add.235
  170.2 2.7 %collective-permute-start.6 = (f32[512,256]{1,0:T(8,128)S(1)}, f32[512,256]{1,0:T(8,128)S(1)}, u32[]{:S(2)}, u32[]{:S(2)}) collective-permute-start(f32[512,256]{1,0:T(8,128)S(1)} %add.235), channel_id=1, source_target_pairs={{1,2},{2,1},{5,6},{6,5},{9,10},{10,9},{13,14},{14,13},{17,18},{18,... | collective-permute-start | bytes 1572872 | tf_op jit(solution)/shard_map/ppermute | solution.py:81
  172.9 1.1 add.243
  174.2 5.0 %fusion.46 = f32[256,4096]{1,0:T(8,128)} fusion(f32[8,4096]{1,0:T(8,128)S(1)} %maximum_select_fusion, s32[]{:T(128)S(6)} %select_n.169), kind=kOutput, calls=%fused_computation.55 | convolution fusion | flops 100663296 | bytes 4333572 | tf_op jit(solution)/shard_map/dot_general | solution.py:101
  179.2 1.1 add.248
  180.3 3.4 %collective-permute-start.19 = (f32[512,256]{1,0:T(8,128)S(1)}, f32[512,256]{1,0:T(8,128)S(1)}, u32[]{:S(2)}, u32[]{:S(2)}) collective-permute-start(f32[512,256]{1,0:T(8,128)S(1)} %copy-done.16), channel_id=1, source_target_pairs={{1,2},{2,1},{5,6},{6,5},{9,10},{10,9},{13,14},{14,13},{17,18},{18,... | collective-permute-start | bytes 1572872 | tf_op jit(solution)/shard_map/ppermute | solution.py:81
  184.6 1.1 add.223
  185.7 12.3 %collective-permute-done.6 = f32[512,256]{1,0:T(8,128)S(1)} collective-permute-done((f32[512,256]{1,0:T(8,128)S(1)}, f32[512,256]{1,0:T(8,128)S(1)}, u32[]{:S(2)}, u32[]{:S(2)}) %collective-permute-start.6) | collective-permute-done | bytes 524320 | tf_op jit(solution)/shard_map/ppermute | solution.py:81
  198.0 3.3 %collective-permute-start.4 = (f32[512,256]{1,0:T(8,128)S(1)}, f32[512,256]{1,0:T(8,128)S(1)}, u32[]{:S(2)}, u32[]{:S(2)}) collective-permute-start(f32[512,256]{1,0:T(8,128)S(1)} %copy-done.14), channel_id=1, source_target_pairs={{1,2},{2,1},{5,6},{6,5},{9,10},{10,9},{13,14},{14,13},{17,18},{18,... | collective-permute-start | bytes 1572872 | tf_op jit(solution)/shard_map/ppermute | solution.py:81
  201.4 2.6 %collective-permute-start.9 = (f32[512,256]{1,0:T(8,128)S(1)}, f32[512,256]{1,0:T(8,128)S(1)}, u32[]{:S(2)}, u32[]{:S(2)}) collective-permute-start(f32[512,256]{1,0:T(8,128)S(1)} %copy-done.15), channel_id=1, source_target_pairs={{1,2},{2,1},{5,6},{6,5},{9,10},{10,9},{13,14},{14,13},{17,18},{18,... | collective-permute-start | bytes 1572872 | tf_op jit(solution)/shard_map/ppermute | solution.py:81
  204.1 5.1 %collective-permute-done.19 = f32[512,256]{1,0:T(8,128)S(1)} collective-permute-done((f32[512,256]{1,0:T(8,128)S(1)}, f32[512,256]{1,0:T(8,128)S(1)}, u32[]{:S(2)}, u32[]{:S(2)}) %collective-permute-start.19) | collective-permute-done | bytes 524320 | tf_op jit(solution)/shard_map/ppermute | solution.py:81
  209.3 11.1 %collective-permute-done.4 = f32[512,256]{1,0:T(8,128)S(1)} collective-permute-done((f32[512,256]{1,0:T(8,128)S(1)}, f32[512,256]{1,0:T(8,128)S(1)}, u32[]{:S(2)}, u32[]{:S(2)}) %collective-permute-start.4) | collective-permute-done | bytes 524320 | tf_op jit(solution)/shard_map/ppermute | solution.py:81
  220.6 10.0 %collective-permute-done.9 = f32[512,256]{1,0:T(8,128)S(1)} collective-permute-done((f32[512,256]{1,0:T(8,128)S(1)}, f32[512,256]{1,0:T(8,128)S(1)}, u32[]{:S(2)}, u32[]{:S(2)}) %collective-permute-start.9) | collective-permute-done | bytes 524320 | tf_op jit(solution)/shard_map/ppermute | solution.py:81
  230.7 1.1 maximum_maximum_fusion
  (78 shorter events, 4.3 us)
Async XLA Ops:
  0.6 79.1 %copy-start = (bf16[3584,64]{0,1:T(8,128)(2,1)S(1)}, bf16[3584,64]{0,1:T(8,128)(2,1)}, u32[]{:S(2)}) copy-start(bf16[3584,64]{0,1:T(8,128)(2,1)} %param.11) | copy-start | bytes 1376260
  2.4 78.6 %collective-permute-start.20 = (f32[512,64]{0,1:T(8,128)S(1)}, f32[512,64]{0,1:T(8,128)}, u32[]{:S(2)}, u32[]{:S(2)}) collective-permute-start(f32[512,64]{0,1:T(8,128)S(1)} %fusion.40), channel_id=1, source_target_pairs={{0,1},{1,0},{2,3},{3,2},{4,5},{5,4},{6,7},{7,6},{8,9},{9,8},{10,11... | collective-permute-start | bytes 393224 | tf_op jit(solution)/shard_map/ppermute | solution.py:22
  18.9 10.1 %copy-start.1 = (bf16[256,3584]{1,0:T(8,128)(2,1)}, bf16[256,3584]{1,0:T(8,128)(2,1)S(1)}, u32[]{:S(2)}) copy-start(bf16[256,3584]{1,0:T(8,128)(2,1)S(1)} %multiply_convert_fusion) | copy-start | bytes 5505028
  23.6 88.2 %collective-permute-start.13 = (f32[512,256]{1,0:T(8,128)}, f32[512,256]{1,0:T(8,128)}, u32[]{:S(2)}, u32[]{:S(2)}) collective-permute-start(f32[512,256]{1,0:T(8,128)} %fusion.20), channel_id=1, source_target_pairs={{0,1},{3,2},{4,5},{7,6},{8,9},{11,10},{12,13},{15,14},{16,17},{19,... | collective-permute-start | bytes 1572872 | tf_op jit(solution)/shard_map/ppermute | solution.py:77
  24.8 5.4 %copy-start.11 = (bf16[512,4096]{1,0:T(8,128)(2,1)S(1)}, bf16[512,4096]{1,0:T(8,128)(2,1)}, u32[]{:S(2)}) copy-start(bf16[512,4096]{1,0:T(8,128)(2,1)} %param.7) | copy-start | bytes 12582916
  29.0 88.6 %collective-permute-start.18 = (f32[512,256]{1,0:T(8,128)}, f32[512,256]{1,0:T(8,128)}, u32[]{:S(2)}, u32[]{:S(2)}) collective-permute-start(f32[512,256]{1,0:T(8,128)} %fusion.4), channel_id=1, source_target_pairs={{0,1},{3,2},{4,5},{7,6},{8,9},{11,10},{12,13},{15,14},{16,17},{19,... | collective-permute-start | bytes 1572872 | tf_op jit(solution)/shard_map/ppermute | solution.py:77
  48.7 74.3 %collective-permute-start.3 = (f32[512,256]{1,0:T(8,128)}, f32[512,256]{1,0:T(8,128)}, u32[]{:S(2)}, u32[]{:S(2)}) collective-permute-start(f32[512,256]{1,0:T(8,128)} %fusion.22), channel_id=1, source_target_pairs={{0,1},{3,2},{4,5},{7,6},{8,9},{11,10},{12,13},{15,14},{16,17},{19,... | collective-permute-start | bytes 1572872 | tf_op jit(solution)/shard_map/ppermute | solution.py:77
  54.0 74.5 %collective-permute-start.8 = (f32[512,256]{1,0:T(8,128)}, f32[512,256]{1,0:T(8,128)}, u32[]{:S(2)}, u32[]{:S(2)}) collective-permute-start(f32[512,256]{1,0:T(8,128)} %fusion.6), channel_id=1, source_target_pairs={{0,1},{3,2},{4,5},{7,6},{8,9},{11,10},{12,13},{15,14},{16,17},{19,... | collective-permute-start | bytes 1572872 | tf_op jit(solution)/shard_map/ppermute | solution.py:77
  75.6 4.2 %copy-start.2 = (bf16[256,3584]{1,0:T(8,128)(2,1)S(1)}, bf16[256,3584]{1,0:T(8,128)(2,1)}, u32[]{:S(2)}) copy-start(bf16[256,3584]{1,0:T(8,128)(2,1)} %copy-done.1) | copy-start | bytes 5505028
  82.6 9.6 %collective-permute-start.21 = (f32[512,64]{0,1:T(8,128)}, f32[512,64]{0,1:T(8,128)}, u32[]{:S(2)}, u32[]{:S(2)}) collective-permute-start(f32[512,64]{0,1:T(8,128)} %add.255), channel_id=1, source_target_pairs={{0,2},{1,3},{2,0},{3,1},{4,6},{5,7},{6,4},{7,5},{8,10},{9,11},{10,... | collective-permute-start | bytes 393224 | tf_op jit(solution)/shard_map/ppermute | solution.py:22
  93.1 0.7 copy-start.10
  96.5 6.8 %collective-permute-start.22 = (f32[2,4096]{1,0:T(2,128)S(1)}, f32[2,4096]{1,0:T(2,128)S(1)}, u32[]{:S(2)}, u32[]{:S(2)}) collective-permute-start(f32[2,4096]{1,0:T(2,128)S(1)} %maximum_multiply_fusion), channel_id=1, source_target_pairs={{0,1},{1,0},{2,3},{3,2},{4,5},{5,4},{6,7},{7,6},{8,9},{9,8},{10,11... | collective-permute-start | bytes 98312 | tf_op jit(solution)/shard_map/ppermute | solution.py:22
  103.4 5.4 %copy-start.13 = (s32[128]{0:T(128)S(1)}, s32[128]{0:T(128)}, u32[]{:S(2)}) copy-start(s32[128]{0:T(128)} %param.13) | copy-start | bytes 1540
  103.4 5.2 %collective-permute-start.23 = (f32[2,4096]{1,0:T(2,128)S(1)}, f32[2,4096]{1,0:T(2,128)S(1)}, u32[]{:S(2)}, u32[]{:S(2)}) collective-permute-start(f32[2,4096]{1,0:T(2,128)S(1)} %fusion.66), channel_id=1, source_target_pairs={{0,2},{1,3},{2,0},{3,1},{4,6},{5,7},{6,4},{7,5},{8,10},{9,11},{10,... | collective-permute-start | bytes 98312 | tf_op jit(solution)/shard_map/ppermute | solution.py:22
  108.7 1.3 collective-permute-start.24
  110.0 7.6 %copy-start.3 = (bf16[256,3584]{1,0:T(8,128)(2,1)S(1)}, bf16[256,3584]{1,0:T(8,128)(2,1)}, u32[]{:S(2)}) copy-start(bf16[256,3584]{1,0:T(8,128)(2,1)} %copy-done.1) | copy-start | bytes 5505028
  110.0 39.4 %collective-permute-start.25 = (f32[4,4096]{1,0:T(4,128)S(1)}, f32[4,4096]{1,0:T(4,128)S(1)}, u32[]{:S(2)}, u32[]{:S(2)}) collective-permute-start(f32[4,4096]{1,0:T(4,128)S(1)} %maximum_select_fusion.1), channel_id=1, source_target_pairs={{0,8},{4,12},{8,0},{12,4},{1,9},{5,13},{9,1},{13,5},{2,10},{6,14},... | collective-permute-start | bytes 196616 | tf_op jit(solution)/shard_map/ppermute | solution.py:30
  116.4 17.9 %collective-permute-start.10 = (f32[512,256]{1,0:T(8,128)S(1)}, f32[512,256]{1,0:T(8,128)S(1)}, u32[]{:S(2)}, u32[]{:S(2)}) collective-permute-start(f32[512,256]{1,0:T(8,128)S(1)} %get-tuple-element.6), channel_id=1, source_target_pairs={{0,1},{3,2},{4,5},{7,6},{8,9},{11,10},{12,13},{15,14},{16,17},{19,... | collective-permute-start | bytes 1572872 | tf_op jit(solution)/shard_map/ppermute | solution.py:77
  121.8 22.5 %collective-permute-start.15 = (f32[512,256]{1,0:T(8,128)S(1)}, f32[512,256]{1,0:T(8,128)S(1)}, u32[]{:S(2)}, u32[]{:S(2)}) collective-permute-start(f32[512,256]{1,0:T(8,128)S(1)} %get-tuple-element.4), channel_id=1, source_target_pairs={{0,1},{3,2},{4,5},{7,6},{8,9},{11,10},{12,13},{15,14},{16,17},{19,... | collective-permute-start | bytes 1572872 | tf_op jit(solution)/shard_map/ppermute | solution.py:77
  127.2 28.3 %collective-permute-start = (f32[512,256]{1,0:T(8,128)S(1)}, f32[512,256]{1,0:T(8,128)S(1)}, u32[]{:S(2)}, u32[]{:S(2)}) collective-permute-start(f32[512,256]{1,0:T(8,128)S(1)} %get-tuple-element.10), channel_id=1, source_target_pairs={{0,1},{3,2},{4,5},{7,6},{8,9},{11,10},{12,13},{15,14},{16,17},{19,... | collective-permute-start | bytes 1572872 | tf_op jit(solution)/shard_map/ppermute | solution.py:77
  132.8 27.9 %copy-start.12 = (f32[16,4096]{1,0:T(8,128)S(1)}, f32[16,4096]{1,0:T(8,128)}, u32[]{:S(2)}) copy-start(f32[16,4096]{1,0:T(8,128)} %param.12) | copy-start | bytes 786436
  132.8 40.1 %copy-start.9 = (f32[512,256]{1,0:T(8,128)S(1)}, f32[512,256]{1,0:T(8,128)}, u32[]{:S(2)}) copy-start(f32[512,256]{1,0:T(8,128)} %fusion.24) | copy-start | bytes 1572868
  132.8 32.9 %collective-permute-start.5 = (f32[512,256]{1,0:T(8,128)}, f32[512,256]{1,0:T(8,128)S(1)}, u32[]{:S(2)}, u32[]{:S(2)}) collective-permute-start(f32[512,256]{1,0:T(8,128)} %get-tuple-element.8), channel_id=1, source_target_pairs={{0,1},{3,2},{4,5},{7,6},{8,9},{11,10},{12,13},{15,14},{16,17},{19,... | collective-permute-start | bytes 1572872 | tf_op jit(solution)/shard_map/ppermute | solution.py:77
  136.1 34.1 %collective-permute-start.11 = (f32[512,256]{1,0:T(8,128)}, f32[512,256]{1,0:T(8,128)}, u32[]{:S(2)}, u32[]{:S(2)}) collective-permute-start(f32[512,256]{1,0:T(8,128)} %add.242), channel_id=1, source_target_pairs={{1,2},{2,1},{5,6},{6,5},{9,10},{10,9},{13,14},{14,13},{17,18},{18,... | collective-permute-start | bytes 1572872 | tf_op jit(solution)/shard_map/ppermute | solution.py:81
  146.2 27.9 %collective-permute-start.16 = (f32[512,256]{1,0:T(8,128)}, f32[512,256]{1,0:T(8,128)}, u32[]{:S(2)}, u32[]{:S(2)}) collective-permute-start(f32[512,256]{1,0:T(8,128)} %add.247), channel_id=1, source_target_pairs={{1,2},{2,1},{5,6},{6,5},{9,10},{10,9},{13,14},{14,13},{17,18},{18,... | collective-permute-start | bytes 1572872 | tf_op jit(solution)/shard_map/ppermute | solution.py:81
  157.4 26.4 %collective-permute-start.1 = (f32[512,256]{1,0:T(8,128)}, f32[512,256]{1,0:T(8,128)}, u32[]{:S(2)}, u32[]{:S(2)}) collective-permute-start(f32[512,256]{1,0:T(8,128)} %add.222), channel_id=1, source_target_pairs={{1,2},{2,1},{5,6},{6,5},{9,10},{10,9},{13,14},{14,13},{17,18},{18,... | collective-permute-start | bytes 1572872 | tf_op jit(solution)/shard_map/ppermute | solution.py:81
  161.1 1.2 collective-permute-start.26
  162.4 18.0 %collective-permute-start.27 = (f32[8,32]{1,0:T(8,128)S(1)}, f32[8,32]{1,0:T(8,128)S(1)}, u32[]{:S(2)}, u32[]{:S(2)}) collective-permute-start(f32[8,32]{1,0:T(8,128)S(1)} %maximum_select_fusion.2), channel_id=1, source_target_pairs={{0,8},{4,12},{8,0},{12,4},{1,9},{5,13},{9,1},{13,5},{2,10},{6,14},... | collective-permute-start | bytes 3080 | tf_op jit(solution)/shard_map/ppermute | solution.py:30
  165.7 13.5 %copy-start.8 = (f32[512,256]{1,0:T(8,128)S(1)}, f32[512,256]{1,0:T(8,128)}, u32[]{:S(2)}) copy-start(f32[512,256]{1,0:T(8,128)} %fusion.8) | copy-start | bytes 1572868
  165.7 35.7 %collective-permute-start.14 = (f32[512,256]{1,0:T(8,128)}, f32[512,256]{1,0:T(8,128)S(1)}, u32[]{:S(2)}, u32[]{:S(2)}) collective-permute-start(f32[512,256]{1,0:T(8,128)} %get-tuple-element.5), channel_id=1, source_target_pairs={{1,2},{2,1},{5,6},{6,5},{9,10},{10,9},{13,14},{14,13},{17,18},{18,... | collective-permute-start | bytes 1572872 | tf_op jit(solution)/shard_map/ppermute | solution.py:81
  170.2 10.2 %copy-start.16 = (f32[512,256]{1,0:T(8,128)S(1)}, f32[512,256]{1,0:T(8,128)}, u32[]{:S(2)}) copy-start(f32[512,256]{1,0:T(8,128)} %get-tuple-element.3) | copy-start | bytes 1572868
  170.2 14.4 %copy-start.6 = (f32[512,256]{1,0:T(8,128)S(1)}, f32[512,256]{1,0:T(8,128)}, u32[]{:S(2)}) copy-start(f32[512,256]{1,0:T(8,128)} %fusion.26) | copy-start | bytes 1572868
  170.2 27.8 %collective-permute-start.6 = (f32[512,256]{1,0:T(8,128)S(1)}, f32[512,256]{1,0:T(8,128)S(1)}, u32[]{:S(2)}, u32[]{:S(2)}) collective-permute-start(f32[512,256]{1,0:T(8,128)S(1)} %add.235), channel_id=1, source_target_pairs={{1,2},{2,1},{5,6},{6,5},{9,10},{10,9},{13,14},{14,13},{17,18},{18,... | collective-permute-start | bytes 1572872 | tf_op jit(solution)/shard_map/ppermute | solution.py:81
  174.0 23.9 %copy-start.14 = (f32[512,256]{1,0:T(8,128)S(1)}, f32[512,256]{1,0:T(8,128)}, u32[]{:S(2)}) copy-start(f32[512,256]{1,0:T(8,128)} %get-tuple-element.9) | copy-start | bytes 1572868
  174.1 27.2 %copy-start.4 = (f32[512,256]{1,0:T(8,128)S(1)}, f32[512,256]{1,0:T(8,128)}, u32[]{:S(2)}) copy-start(f32[512,256]{1,0:T(8,128)} %fusion.10) | copy-start | bytes 1572868
  174.1 27.3 %copy-start.15 = (f32[512,256]{1,0:T(8,128)S(1)}, f32[512,256]{1,0:T(8,128)}, u32[]{:S(2)}) copy-start(f32[512,256]{1,0:T(8,128)} %get-tuple-element.7) | copy-start | bytes 1572868
  174.1 29.9 %copy-start.7 = (f32[512,256]{1,0:T(8,128)S(1)}, f32[512,256]{1,0:T(8,128)}, u32[]{:S(2)}) copy-start(f32[512,256]{1,0:T(8,128)} %fusion.28) | copy-start | bytes 1572868
  174.1 29.8 %collective-permute-start.12 = (f32[512,256]{1,0:T(8,128)S(1)}, f32[512,256]{1,0:T(8,128)S(1)}, u32[]{:S(2)}, u32[]{:S(2)}) collective-permute-start(f32[512,256]{1,0:T(8,128)S(1)} %add.243), channel_id=1, source_target_pairs={{0,1},{2,3},{1,0},{3,2},{4,5},{6,7},{5,4},{7,6},{8,9},{10,11},{9,8... | collective-permute-start | bytes 1572872 | tf_op jit(solution)/shard_map/ppermute | solution.py:77
  180.3 40.1 %copy-start.5 = (f32[512,256]{1,0:T(8,128)S(1)}, f32[512,256]{1,0:T(8,128)}, u32[]{:S(2)}) copy-start(f32[512,256]{1,0:T(8,128)} %fusion.30) | copy-start | bytes 1572868
  180.3 28.9 %collective-permute-start.19 = (f32[512,256]{1,0:T(8,128)S(1)}, f32[512,256]{1,0:T(8,128)S(1)}, u32[]{:S(2)}, u32[]{:S(2)}) collective-permute-start(f32[512,256]{1,0:T(8,128)S(1)} %copy-done.16), channel_id=1, source_target_pairs={{1,2},{2,1},{5,6},{6,5},{9,10},{10,9},{13,14},{14,13},{17,18},{18,... | collective-permute-start | bytes 1572872 | tf_op jit(solution)/shard_map/ppermute | solution.py:81
  183.8 25.4 %collective-permute-start.17 = (f32[512,256]{1,0:T(8,128)S(1)}, f32[512,256]{1,0:T(8,128)S(1)}, u32[]{:S(2)}, u32[]{:S(2)}) collective-permute-start(f32[512,256]{1,0:T(8,128)S(1)} %add.248), channel_id=1, source_target_pairs={{0,1},{2,3},{1,0},{3,2},{4,5},{6,7},{5,4},{7,6},{8,9},{10,11},{9,8... | collective-permute-start | bytes 1572872 | tf_op jit(solution)/shard_map/ppermute | solution.py:77
  198.0 22.5 %collective-permute-start.4 = (f32[512,256]{1,0:T(8,128)S(1)}, f32[512,256]{1,0:T(8,128)S(1)}, u32[]{:S(2)}, u32[]{:S(2)}) collective-permute-start(f32[512,256]{1,0:T(8,128)S(1)} %copy-done.14), channel_id=1, source_target_pairs={{1,2},{2,1},{5,6},{6,5},{9,10},{10,9},{13,14},{14,13},{17,18},{18,... | collective-permute-start | bytes 1572872 | tf_op jit(solution)/shard_map/ppermute | solution.py:81
  201.4 29.2 %collective-permute-start.9 = (f32[512,256]{1,0:T(8,128)S(1)}, f32[512,256]{1,0:T(8,128)S(1)}, u32[]{:S(2)}, u32[]{:S(2)}) collective-permute-start(f32[512,256]{1,0:T(8,128)S(1)} %copy-done.15), channel_id=1, source_target_pairs={{1,2},{2,1},{5,6},{6,5},{9,10},{10,9},{13,14},{14,13},{17,18},{18,... | collective-permute-start | bytes 1572872 | tf_op jit(solution)/shard_map/ppermute | solution.py:81
  203.9 16.5 %collective-permute-start.2 = (f32[512,256]{1,0:T(8,128)S(1)}, f32[512,256]{1,0:T(8,128)S(1)}, u32[]{:S(2)}, u32[]{:S(2)}) collective-permute-start(f32[512,256]{1,0:T(8,128)S(1)} %add.223), channel_id=1, source_target_pairs={{0,1},{2,3},{1,0},{3,2},{4,5},{6,7},{5,4},{7,6},{8,9},{10,11},{9,8... | collective-permute-start | bytes 1572872 | tf_op jit(solution)/shard_map/ppermute | solution.py:77
  209.2 21.4 %collective-permute-start.7 = (f32[512,256]{1,0:T(8,128)S(1)}, f32[512,256]{1,0:T(8,128)S(1)}, u32[]{:S(2)}, u32[]{:S(2)}) collective-permute-start(f32[512,256]{1,0:T(8,128)S(1)} %add.236), channel_id=1, source_target_pairs={{0,1},{2,3},{1,0},{3,2},{4,5},{6,7},{5,4},{7,6},{8,9},{10,11},{9,8... | collective-permute-start | bytes 1572872 | tf_op jit(solution)/shard_map/ppermute | solution.py:77

commit v2 on v0

v2 whole, which is shorter than its diff:
```python
import functools
import math

import jax
import jax.numpy as jnp
from jax import lax
from jax.experimental import pallas as pl
from jax.experimental.pallas import tpu as pltpu
from jax.sharding import PartitionSpec as P

LEN = 256
SK = 4096
HIGH = lax.Precision.HIGHEST
VMEM = 60 << 20
BRIEF = pl.CostEstimate(flops=1, bytes_accessed=1, transcendentals=0)


def widest(size, choices):
    return next(c for c in choices if size % c == 0)


def front_kernel(feat, picks, extra, block_ref, tok_ref, w_ref, act_ref, *refs):
    pieces = [(k, own, feat // split, r) for k, own, split in picks for r in range(split)]
    grad_ref, part_refs = refs[-1 - len(pieces)], refs[len(refs) - len(pieces):]

    @pl.when(pl.program_id(0) == 0)
    def _():
        for part_ref in part_refs:
            part_ref[...] = jnp.zeros_like(part_ref)
        if extra:
            cols_ref, proj_ref = refs[:2]
            factor = lax.dot_general(
                proj_ref[...], cols_ref[...], (((1,), (1,)), ((), ())), preferred_element_type=jnp.float32
            )
            for d in range(factor.shape[1] // LEN):
                at = slice(d * factor.shape[0], (d + 1) * factor.shape[0])
                part_refs[-1][at, :] = factor[:, d * LEN:(d + 1) * LEN]

    preact = jnp.dot(tok_ref[...], w_ref[...], preferred_element_type=jnp.float32)
    sig = 1.0 / (1.0 + jnp.exp(-preact))
    slopes = sig * (1.0 + preact * (1.0 - sig))
    grad = (act_ref[...].astype(jnp.float32) * slopes).astype(jnp.bfloat16).T
    grad_ref[...] = grad
    for part_ref, (k, own, rows, r) in zip(part_refs, pieces):
        start = pl.multiple_of(block_ref[k] * feat + r * rows, rows)
        right = grad if own else refs[0][...]
        part_ref[part_ref.shape[0] - rows:, :] += jnp.dot(w_ref[pl.ds(start, rows), :], right, preferred_element_type=jnp.float32)


def front(doc, blocks, picks, tokens, weight, grad_act, other, proj_in, feat, earlier):
    width, hidden = weight.shape
    cols = widest(hidden, (512, 256, 128))
    rows = [feat // split for _, _, split in picks for _ in range(split)]
    more, more_specs = list(other), [pl.BlockSpec((cols, LEN), lambda j, b: (j, 0))] * len(other)
    if proj_in is not None:
        more = [tokens, proj_in]
        more_specs = [
            pl.BlockSpec((tokens.shape[0], feat), lambda j, b: (0, b[len(picks)])),
            pl.BlockSpec(proj_in.shape, lambda j, b: (0, 0)),
        ]
        rows[-1] += tokens.shape[0] // LEN * proj_in.shape[0]
    return pl.pallas_call(
        functools.partial(front_kernel, feat, picks, proj_in is not None),
        grid_spec=pltpu.PrefetchScalarGridSpec(
            num_scalar_prefetch=1,
            grid=(hidden // cols,),
            in_specs=[
                pl.BlockSpec((LEN, width), lambda j, b: (doc, 0)),
                pl.BlockSpec((width, cols), lambda j, b: (0, j)),
                pl.BlockSpec((LEN, cols), lambda j, b: (doc, j)),
            ]
            + more_specs
            + [pl.BlockSpec(memory_space=pl.ANY)] * len(earlier),
            out_specs=[pl.BlockSpec((cols, LEN), lambda j, b: (j, 0))]
            + [pl.BlockSpec((size, LEN), lambda j, b: (0, 0)) for size in rows],
        ),
        out_shape=[jax.ShapeDtypeStruct((hidden, LEN), jnp.bfloat16)]
        + [jax.ShapeDtypeStruct((size, LEN), jnp.float32) for size in rows],
        compiler_params=pltpu.CompilerParams(vmem_limit_bytes=VMEM),
        cost_estimate=BRIEF,
    )(blocks, tokens, weight, grad_act, *more, *earlier)


def sketch_kernel(widths, proj_ref, in_ref, *refs):
    grads, out_ref = refs[: len(widths)], refs[-1]
    parts = [jnp.dot(proj_ref[...], grad[...], preferred_element_type=jnp.float32) for grad in grads]
    factor_out = jnp.concatenate(parts, 1)
    size = out_ref.shape[2]
    for d in range(out_ref.shape[0]):
        out_ref[d] = lax.dot_general(
            factor_out[:, d * LEN:(d + 1) * LEN],
            in_ref[d * size:(d + 1) * size, :],
            (((1,), (1,)), ((), ())),
            precision=HIGH,
            preferred_element_type=jnp.float32,
        ) / math.sqrt(LEN)


def sketch(proj_out, factor_in, grads, earlier):
    widths = tuple(grad.shape[1] for grad in grads)
    docs = sum(widths) // LEN
    return pl.pallas_call(
        functools.partial(sketch_kernel, widths),
        in_specs=[pl.BlockSpec(memory_space=pltpu.VMEM)] * (2 + len(grads))
        + [pl.BlockSpec(memory_space=pl.ANY)] * len(earlier),
        out_specs=pl.BlockSpec(memory_space=pltpu.VMEM),
        out_shape=jax.ShapeDtypeStruct((docs, proj_out.shape[0], factor_in.shape[0] // docs), jnp.float32),
        compiler_params=pltpu.CompilerParams(vmem_limit_bytes=VMEM),
        cost_estimate=BRIEF,
    )(proj_out, factor_in, *grads, *earlier)


def line_pairs(count, step, color):
    up = [(i, i + 1) for i in range(count - 1) if i < step and i % 2 == color]
    down = [(j, j - 1) for j in range(1, count) if count - 1 - j < step and (j - 1) % 2 == color]
    return up + down


class Total:
    def __init__(self, own, count, hops=()):
        self.own, self.count, self.hops = own, count, list(hops)

    def hop(self):
        step = len(self.hops) + 1
        send = self.own + self.hops[-1] if self.hops else self.own
        pairs = [(step - 1, step), (self.count - step, self.count - step - 1)]
        self.hops.append(lax.ppermute(send, "tensor", pairs))
        return self.hops[-1]

    def result(self):
        return functools.reduce(jnp.add, self.hops, self.own)


def gram_kernel(mine_ref, all_ref, *refs):
    refs[-1][...] = lax.dot_general(
        mine_ref[...], all_ref[...], (((0,), (0,)), ((), ())), precision=HIGH, preferred_element_type=jnp.float32
    )


def gram_rows_of(mine, everyone, earlier):
    docs, rows = mine.shape
    width = everyone.shape[1]
    cols = min(1024, width)
    return pl.pallas_call(
        gram_kernel,
        grid=(width // cols,),
        in_specs=[pl.BlockSpec((docs, rows), lambda j: (0, 0)), pl.BlockSpec((docs, cols), lambda j: (0, j))]
        + [pl.BlockSpec(memory_space=pl.ANY)] * len(earlier),
        out_specs=pl.BlockSpec((rows, cols), lambda j: (0, j)),
        out_shape=jax.ShapeDtypeStruct((rows, width), jnp.float32),
        compiler_params=pltpu.CompilerParams(vmem_limit_bytes=VMEM),
        cost_estimate=BRIEF,
    )(mine, everyone, *earlier)


def after(x, *others):
    return lax.optimization_barrier((x, *others))[0]


SPLITS = (1, 1)


class Line:
    def __init__(self, count):
        self.count = count
        self.blocks = {}
        self.received = {}
        self.sums = {}

    def sum_of(self, step, color, doc, r):
        place = (step, color, doc, r)
        if place not in self.sums:
            block = self.blocks[step if color == 0 else self.count - step, doc, r]
            before = self.send(step - 1, 1 - color, doc, r)
            self.sums[place] = block + before[0] if before else block
        return self.sums[place]

    def send(self, step, color, doc, r):
        place = (step, color, doc, r)
        if place not in self.received and line_pairs(self.count, step, color):
            block = self.sum_of(*place)
            self.received[place] = lax.ppermute(block, "tensor", line_pairs(self.count, step, color))
        return [self.received[place]] if place in self.received else []


def body(tokens, weight, grad_act, proj_in, proj_out, query_bank, query_index):
    n = lax.axis_size("tensor")
    m = lax.axis_size("dp")
    pos = lax.axis_index("tensor")
    dp_pos = lax.axis_index("dp")
    docs = tokens.shape[0] // LEN
    feat = proj_in.shape[0]
    sign = jnp.where(pos % 2 == 0, -1, 1)
    line = Line(n)
    order = (pos + sign * jnp.arange(n, dtype=jnp.int32)) % n

    def make(doc, blocks, picks, other, proj):
        return front(doc, blocks, picks, tokens, weight, grad_act, other, proj, feat, [])

    short = n == 4
    inner = (pos > 0) & (pos < n - 1) & short
    held = (pos + sign * (jnp.arange(2, dtype=jnp.int32) + 1 + jnp.where(inner, jnp.array([1, -1], jnp.int32), 0))) % n
    held = jnp.concatenate([held, pos.astype(jnp.int32).reshape(1)])
    grad, near, far = make(0, held, [(0, True, 1), (1, True, 1)], [], proj_in.T)
    size = far.shape[0] - feat
    near_in, far_in = (lax.ppermute(x, "tensor", line_pairs(n, 1, 0)) for x in (near, far))
    for k, block, arrived in ((1, near, near_in), (2, far[size:], far_in[size:])):
        line.blocks[k, 0, 0], line.received[k, 0, 0, 0] = block, arrived
    picks = [(k % n, True, 1) for k in range(1, n + 1)] + [(k % n, False, 1) for k in range(3, n + 1)]
    other, *parts = make(1, order, picks, [grad], None)
    for (k, own, _), part in zip(picks, parts):
        line.blocks[k, 1 if own else 0, 0] = part
    grads = [grad, other]
    factor_in = Total(far[:size], n, [far_in[:size]])
    if short:
        line.received[2, 1, 0, 0] = lax.ppermute(near + after(near_in, other), "tensor", line_pairs(n, 2, 1))
        far_sum = far + after(far_in, other)
        passed = lax.ppermute(far_sum, "tensor", line_pairs(n, 3, 1))
        line.received[3, 1, 0, 0] = passed[size:]
        factor_in.hops.append(passed[:size])
        line.received[1, 0, 1, 0] = after(line.send(1, 0, 1, 0)[0], far_sum)
        line.received[2, 0, 1, 0] = after(line.send(2, 0, 1, 0)[0], line.sum_of(3, 0, 0, 0))
    while len(factor_in.hops) + 1 < n:
        factor_in.hop()

    def gate(x, *places):
        return after(x, *(line.send(*place)[0] for place in places)) if short else x

    sketches = sketch(proj_out.T, factor_in.result(), grads, []).reshape(docs, SK)
    others = [lax.ppermute(sketches, "tensor", [(i, i ^ far) for i in range(n)]) for far in range(1, n)]
    own = gate(functools.reduce(jnp.add, others, sketches), (3, 0, 0, 0))
    if short:
        own = after(own, line.sum_of(3, 1, 1, 0), line.sum_of(3, 0, 1, 0))
    others = [lax.ppermute(own, "dp", [(i, i ^ far) for i in range(m)]) for far in range(1, m)]
    everyone = jnp.concatenate([own, *others], 0)
    gram_rows = SK // (m * n)
    mine = lax.dynamic_slice_in_dim(everyone, (dp_pos * n + pos) * gram_rows, gram_rows, 1)
    gram = gram_rows_of(mine, everyone, [])
    scores = lax.dot_general(everyone, query_bank, (((1,), (1,)), ((), ())), precision=HIGH) / math.sqrt(SK)
    scores = after(scores, gram)
    parts = [scores[:docs]]
    for far in range(1, m):
        parts.append(lax.ppermute(scores[far * docs:(far + 1) * docs], "dp", [(i, i ^ far) for i in range(m)]))
    scores = jnp.concatenate(parts, 1)
    bank = query_bank.shape[0]
    places = jnp.concatenate([(dp_pos ^ far) * bank + jnp.arange(bank, dtype=query_index.dtype) for far in range(m)])
    for step in range(1, n):
        for doc in range(docs):
            for r in range(SPLITS[doc]):
                line.send(step, 0, doc, r)
                line.send(step, 1, doc, r)

    outs = [[] for _ in range(docs)]
    for doc in range(docs):
        for r in range(SPLITS[doc]):
            total = line.blocks[0, doc, r]
            last = [line.received[n - 1, color, doc, r] for color in (1, 0) if (n - 1, color, doc, r) in line.received]
            for part in lax.optimization_barrier((*last, scores))[:-1] if short and doc == docs - 1 else last:
                total = total + part
            outs[doc].append(total.astype(jnp.bfloat16))
    grad_in_t = jnp.concatenate([jnp.concatenate(row, 0) for row in outs], 1)

    picked = jnp.where(query_index[None, :, None] == places[None, None, :], scores[:, None, :], 0.0)
    return (grad_in_t, gram, jnp.sum(picked, -1))


def solution(mesh):
    in_specs = (
        P(("groups", "dp"), None),
        P(None, "tensor"),
        P(("groups", "dp"), "tensor"),
        P("tensor", None),
        P("tensor", None),
        P(("groups", "dp"), None),
        P("groups"),
    )
    out_specs = (
        P("tensor", ("groups", "dp")),
        P(("groups", "dp", "tensor"), None),
        P(("groups", "dp"), None),
    )
    return jax.shard_map(body, mesh=mesh, in_specs=in_specs, out_specs=out_specs, check_vma=False)
```

time: 362 us -> 182 us (0.50)
  waiting for transfers between devices: 255 us -> 65.9 us
  matrix products: 77 us -> 1.23 us
  Pallas kernels: 0 us -> 60.4 us
  starting transfers between devices: 0.35 us -> 24.7 us
  other arithmetic: 2.52 us -> 23.1 us
  between operations: 15.3 us -> 0.9 us
  local copies, waits for them, and re-layouts: 10 us -> 3.26 us
    reduce_scatter x2 -> x0, waiting for transfers between devices: 246 us -> none  [the longest x1 126 us: body(): lax.psum_scatter(jnp.dot(picked.T, sketches, precision=lax.Precision.HIGH...]
    dot_general x7 -> x1, matrix products: 77 us -> 1.23 us  [body(): lax.dot_general(everyone, query_bank, (((1,), (1,)), ((), ())), precision...]
    ppermute x0 -> x20, waiting for transfers between devices: none -> 65.9 us  [the longest x6 32.6 us: send(): lax.ppermute(block, 'tensor', line_pairs(self.count, step, color))]
    pallas_call x0 -> x4, Pallas kernels: none -> 60.4 us  [the longest x2 50.5 us: front(): pl.pallas_call(functools.partial(front_kernel, feat, picks, proj_in is no...]
    ppermute x0 -> x20, starting transfers between devices: none -> 24.7 us  [the longest x6 8.02 us: send(): lax.ppermute(block, 'tensor', line_pairs(self.count, step, color))]
    add x0 -> x11, other arithmetic: none -> 15.4 us  [the longest x4 8.87 us: sum_of(): self.sums[place] = block + before[0] if before else block]
    psum x1 -> x0, waiting for transfers between devices: 8.03 us -> none  [body(): factors = lax.psum(jnp.concatenate([part_in, part_out], axis=1), 'tensor')]
    gather x2 -> x0, local copies, waits for them, and re-layouts: 6.32 us -> none  [the longest x1 3.51 us: body(): chosen = jnp.take(queries, query_index, axis=0)]
  transfers between devices with their start and end apart: 4 -> 20, of which waited for: 3 -> 10; matrix products, arithmetic and copies ran while one was open for 16% -> 13% of each run, Pallas kernels for 0% -> 22%
where the time goes in v2:
time: 182 us; the launch traced here: 180 us
  waiting for transfers between devices  65.9 us (36%)
  Pallas kernels  60.4 us (33%)
  starting transfers between devices  24.7 us (14%)
  other arithmetic  23.1 us (13%)
  local copies, waits for them, and re-layouts  3.26 us (2%)
    pallas_call x2, Pallas kernels, front(): pl.pallas_call(functools.partial(front_kernel, feat, picks, proj_in is no...  50.5 us
    ppermute x6, waiting for transfers between devices, send(): lax.ppermute(block, 'tensor', line_pairs(self.count, step, color))  32.6 us
    ppermute x2, waiting for transfers between devices, body(): lax.ppermute(x, 'tensor', line_pairs(n, 1, 0))  15.4 us
    add x4, other arithmetic, sum_of(): self.sums[place] = block + before[0] if before else block  8.87 us
    ppermute x3, waiting for transfers between devices, body(): lax.ppermute(sketches, 'tensor', [(i, i ^ far) for i in range(n)])  8.04 us
    ppermute x6, starting transfers between devices, send(): lax.ppermute(block, 'tensor', line_pairs(self.count, step, color))  8.02 us
    ppermute x1, waiting for transfers between devices, body(): lax.ppermute(near + after(near_in, other), 'tensor', line_pairs(n, 2, 1))  7.36 us
    pallas_call x1, Pallas kernels, gram_rows_of(): pl.pallas_call(gram_kernel, grid=(width // cols,), in_specs=[pl.BlockSpec...  5.97 us
  transfers between devices with their start and end apart: 20, of which 10 were waited for; matrix products, arithmetic and copies ran while one was open for 13% of the time, Pallas kernels for 22%

profile of v2, /device:TPU:16, one launch (start us, length us, event | category | flops | bytes accessed | tf_op | source)
XLA Modules:
  0.0 179.6 jit_solution(10304132745223900282)
XLA Ops:
  0.6 0.0 copy-start
  0.7 0.7 and_select_fusion
  1.4 0.6 pad_add_fusion.block_ref
  2.0 21.3 %shard_map.103 = (bf16[3584,256]{1,0:T(8,128)(2,1)}, f32[1024,256]{1,0:T(8,128)}, f32[1152,256]{1,0:T(8,128)}) custom-call(s32[3]{0:T(128)} %pad_add_fusion.block_ref, bf16[512,4096]{1,0:T(8,128)(2,1)} %tok_ref.3, bf16[4096,3584]{1,0:T(8,128)(2,1)} %w_ref.3, bf16[512,3584]{1,0:T(8,128)(2,1)} %act_ref.3, bf16[512,4096]{1,0:T(8,128)(2,1)} %tok_ref.3, ...), custom_call_target="tpu_custom_call" | custom-call | flops 1 | bytes 1 | tf_op jit(solution)/shard_map/pallas_call | solution.py:62
  23.3 1.3 collective-permute-start
  24.6 1.3 collective-permute-start.2
  25.9 0.5 and_select_fusion.1.block_ref
  26.4 29.2 %shard_map.104 = (bf16[3584,256]{1,0:T(8,128)(2,1)}, f32[1024,256]{1,0:T(8,128)}, f32[1024,256]{1,0:T(8,128)}, f32[1024,256]{1,0:T(8,128)}, f32[1024,256]{1,0:T(...) custom-call(s32[4]{0:T(128)} %and_select_fusion.1.block_ref, bf16[512,4096]{1,0:T(8,128)(2,1)} %tok_ref.3, ...), custom_call_target="tpu_custom_call" | custom-call | flops 1 | bytes 1 | tf_op jit(solution)/shard_map/pallas_call | solution.py:62
  55.6 1.3 collective-permute-start.7
  56.9 1.0 copy-done.2
  57.9 1.2 add.124
  59.1 2.3 %collective-permute-start.1 = (f32[1152,256]{1,0:T(8,128)}, f32[1152,256]{1,0:T(8,128)S(1)}, u32[]{:S(2)}, u32[]{:S(2)}) collective-permute-start(f32[1152,256]{1,0:T(8,128)} %add.124), channel_id=1, source_target_pairs={{1,2},{2,1},{5,6},{6,5},{9,10},{10,9},{13,14},{14,13},{17,18},{18,... | collective-permute-start | bytes 3538952 | tf_op jit(solution)/shard_map/ppermute | solution.py:218
  61.4 15.4 %collective-permute-done.2 = f32[1024,256]{1,0:T(8,128)} collective-permute-done((f32[1024,256]{1,0:T(8,128)}, f32[1024,256]{1,0:T(8,128)}, u32[]{:S(2)}, u32[]{:S(2)}) %collective-permute-start.2) | collective-permute-done | bytes 1048608 | tf_op jit(solution)/shard_map/ppermute | solution.py:206
  76.8 2.4 %add.126 = f32[1024,256]{1,0:T(8,128)} add(f32[1024,256]{1,0:T(8,128)S(1)} %copy-done.7, f32[1024,256]{1,0:T(8,128)} %collective-permute-done.2) | non-fusion elementwise | flops 262144 | bytes 3145728 | tf_op jit(solution)/shard_map/add | solution.py:216
  79.2 2.3 %collective-permute-start.3 = (f32[1024,256]{1,0:T(8,128)}, f32[1024,256]{1,0:T(8,128)}, u32[]{:S(2)}, u32[]{:S(2)}) collective-permute-start(f32[1024,256]{1,0:T(8,128)} %add.126), channel_id=1, source_target_pairs={{1,2},{2,1},{5,6},{6,5},{9,10},{10,9},{13,14},{14,13},{17,18},{18,... | collective-permute-start | bytes 3145736 | tf_op jit(solution)/shard_map/ppermute | solution.py:216
  81.5 1.3 collective-permute-start.5
  82.8 16.4 %collective-permute-done.7 = f32[1024,256]{1,0:T(8,128)S(1)} collective-permute-done((f32[1024,256]{1,0:T(8,128)}, f32[1024,256]{1,0:T(8,128)S(1)}, u32[]{:S(2)}, u32[]{:S(2)}) %collective-permute-start.7) | collective-permute-done | bytes 1048608 | tf_op jit(solution)/shard_map/ppermute | solution.py:182
  99.2 2.3 %add.130 = f32[1024,256]{1,0:T(8,128)} add(f32[1024,256]{1,0:T(8,128)} %get-tuple-element.32, f32[1024,256]{1,0:T(8,128)S(1)} %collective-permute-done.7) | non-fusion elementwise | flops 262144 | bytes 3145728 | tf_op jit(solution)/shard_map/add | solution.py:175
  101.5 2.3 %collective-permute-start.8 = (f32[1024,256]{1,0:T(8,128)}, f32[1024,256]{1,0:T(8,128)}, u32[]{:S(2)}, u32[]{:S(2)}) collective-permute-start(f32[1024,256]{1,0:T(8,128)} %add.130), channel_id=1, source_target_pairs={{1,2},{2,1},{5,6},{6,5},{9,10},{10,9},{13,14},{14,13},{17,18},{18,... | collective-permute-start | bytes 3145736 | tf_op jit(solution)/shard_map/ppermute | solution.py:182
  103.9 0.0 collective-permute-done.1
  103.9 1.3 collective-permute-start.10
  105.2 7.4 %collective-permute-done.3 = f32[1024,256]{1,0:T(8,128)} collective-permute-done((f32[1024,256]{1,0:T(8,128)}, f32[1024,256]{1,0:T(8,128)}, u32[]{:S(2)}, u32[]{:S(2)}) %collective-permute-start.3) | collective-permute-done | bytes 1048608 | tf_op jit(solution)/shard_map/ppermute | solution.py:216
  112.6 2.7 %add.127 = f32[1024,256]{1,0:T(8,128)} add(f32[1024,256]{1,0:T(8,128)} %get-tuple-element.27, f32[1024,256]{1,0:T(8,128)} %collective-permute-done.3) | non-fusion elementwise | flops 262144 | bytes 3145728 | tf_op jit(solution)/shard_map/add | solution.py:175
  115.3 0.0 collective-permute-start.4
  115.3 0.0 collective-permute-done.10
  115.3 1.6 fusion.3.in_ref
  116.9 3.9 %shard_map.105 = f32[2,64,64]{2,1,0:T(8,128)} custom-call(bf16[64,3584]{1,0:T(8,128)(2,1)} %bitcast.4, f32[128,256]{1,0:T(8,128)} %fusion.3.in_ref, bf16[3584,256]{1,0:T(8,128)(2,1)} %get-tuple-element.22.refs_0_, bf16[3584,256]{1,0:T(8,128)(2,1)} %get-tuple-element.25.refs_1_), custom_call_target="tpu_custom_call" | custom-call | flops 1 | bytes 1 | tf_op jit(solution)/shard_map/pallas_call | solution.py:102
  120.8 1.5 reshape.46
  122.4 0.4 collective-permute-start.13
  122.8 3.9 %collective-permute-start.12 = (f32[2,4096]{1,0:T(2,128)}, f32[2,4096]{1,0:T(2,128)S(1)}, u32[]{:S(2)}, u32[]{:S(2)}) collective-permute-start(f32[2,4096]{1,0:T(2,128)} %reshape.46), channel_id=1, source_target_pairs={{0,2},{1,3},{2,0},{3,1},{4,6},{5,7},{6,4},{7,5},{8,10},{9,11},{10,... | collective-permute-start | bytes 98312 | tf_op jit(solution)/shard_map/ppermute | solution.py:230
  126.7 0.0 collective-permute-start.11
  126.7 0.1 pad_add_fusion.1
  126.8 1.5 add.129
  128.3 6.3 %collective-permute-done.8 = f32[1024,256]{1,0:T(8,128)} collective-permute-done((f32[1024,256]{1,0:T(8,128)}, f32[1024,256]{1,0:T(8,128)}, u32[]{:S(2)}, u32[]{:S(2)}) %collective-permute-start.8) | collective-permute-done | bytes 1048608 | tf_op jit(solution)/shard_map/ppermute | solution.py:182
  134.6 2.4 %add.131 = f32[1024,256]{1,0:T(8,128)} add(f32[1024,256]{1,0:T(8,128)S(1)} %copy-done.5, f32[1024,256]{1,0:T(8,128)} %collective-permute-done.8) | non-fusion elementwise | flops 262144 | bytes 3145728 | tf_op jit(solution)/shard_map/add | solution.py:175
  137.0 0.0 collective-permute-done.13
  137.0 7.6 %collective-permute-done.12 = f32[2,4096]{1,0:T(2,128)S(1)} collective-permute-done((f32[2,4096]{1,0:T(2,128)}, f32[2,4096]{1,0:T(2,128)S(1)}, u32[]{:S(2)}, u32[]{:S(2)}) %collective-permute-start.12) | collective-permute-done | bytes 32800 | tf_op jit(solution)/shard_map/ppermute | solution.py:230
  144.6 0.5 collective-permute-done.11
  145.1 1.4 add_add_fusion
  146.5 0.2 collective-permute-start.16
  146.6 1.4 collective-permute-start.15
  148.0 0.3 collective-permute-start.14
  148.3 0.1 broadcast_compare_fusion
  148.4 3.0 %collective-permute-start.6 = (f32[1024,256]{1,0:T(8,128)S(1)}, f32[1024,256]{1,0:T(8,128)}, u32[]{:S(2)}, u32[]{:S(2)}) collective-permute-start(f32[1024,256]{1,0:T(8,128)S(1)} %add.129), channel_id=1, source_target_pairs={{1,2},{2,1},{5,6},{6,5},{9,10},{10,9},{13,14},{14,13},{17,18},{18,... | collective-permute-start | bytes 3145736 | tf_op jit(solution)/shard_map/ppermute | solution.py:182
  151.5 0.1 collective-permute-start.9
  151.5 0.0 collective-permute-done.16
  151.6 0.0 collective-permute-done.14
  151.6 0.9 pad_maximum_fusion.1.all_ref
  152.5 0.6 constant_dynamic-slice_fusion.mine_ref
  153.1 0.0 copy-done.8
  153.1 1.4 fusion.1
  154.5 6.0 %shard_map.106 = f32[256,4096]{1,0:T(8,128)} custom-call(f32[8,256]{1,0:T(8,128)} %constant_dynamic-slice_fusion.mine_ref, f32[8,4096]{1,0:T(8,128)} %copy-done.8), custom_call_target="tpu_custom_call" | custom-call | flops 1 | bytes 1 | tf_op jit(solution)/shard_map/pallas_call | solution.py:144
  160.5 1.2 convolution_multiply_fusion
  161.7 0.9 collective-permute-start.19
  162.6 0.8 collective-permute-start.18
  163.4 0.3 collective-permute-start.17
  163.7 1.1 collective-permute-done.19
  164.8 1.4 collective-permute-done.18
  166.2 0.1 pad_maximum_fusion.2
  166.3 0.7 select_reduce_fusion
  166.9 8.7 %collective-permute-done.6 = f32[1024,256]{1,0:T(8,128)} collective-permute-done((f32[1024,256]{1,0:T(8,128)S(1)}, f32[1024,256]{1,0:T(8,128)}, u32[]{:S(2)}, u32[]{:S(2)}) %collective-permute-start.6) | collective-permute-done | bytes 1048608 | tf_op jit(solution)/shard_map/ppermute | solution.py:182
  175.7 1.1 collective-permute-done.9
  176.8 1.7 add_convert_fusion
  178.5 1.1 pad_maximum_fusion
  (26 shorter events, 0.1 us)
Async XLA Ops:
  0.6 159.9 %copy-start = (f32[16,4096]{1,0:T(8,128)S(1)}, f32[16,4096]{1,0:T(8,128)}, u32[]{:S(2)}) copy-start(f32[16,4096]{1,0:T(8,128)} %param.13) | copy-start | bytes 786436
  23.3 33.6 %collective-permute-start = (f32[1152,256]{1,0:T(8,128)}, f32[1152,256]{1,0:T(8,128)S(1)}, u32[]{:S(2)}, u32[]{:S(2)}) collective-permute-start(f32[1152,256]{1,0:T(8,128)} %get-tuple-element.24), channel_id=1, source_target_pairs={{0,1},{3,2},{4,5},{7,6},{8,9},{11,10},{12,13},{15,14},{16,17},{19,... | collective-permute-start | bytes 3538952 | tf_op jit(solution)/shard_map/ppermute | solution.py:206
  24.6 52.2 %collective-permute-start.2 = (f32[1024,256]{1,0:T(8,128)}, f32[1024,256]{1,0:T(8,128)}, u32[]{:S(2)}, u32[]{:S(2)}) collective-permute-start(f32[1024,256]{1,0:T(8,128)} %get-tuple-element.28), channel_id=1, source_target_pairs={{0,1},{3,2},{4,5},{7,6},{8,9},{11,10},{12,13},{15,14},{16,17},{19,... | collective-permute-start | bytes 3145736 | tf_op jit(solution)/shard_map/ppermute | solution.py:206
  26.4 31.5 %copy-start.1 = (f32[1152,256]{1,0:T(8,128)S(1)}, f32[1152,256]{1,0:T(8,128)}, u32[]{:S(2)}) copy-start(f32[1152,256]{1,0:T(8,128)} %get-tuple-element.24) | copy-start | bytes 3538948
  55.6 43.6 %collective-permute-start.7 = (f32[1024,256]{1,0:T(8,128)}, f32[1024,256]{1,0:T(8,128)S(1)}, u32[]{:S(2)}, u32[]{:S(2)}) collective-permute-start(f32[1024,256]{1,0:T(8,128)} %get-tuple-element.31), channel_id=1, source_target_pairs={{0,1},{3,2},{4,5},{7,6},{8,9},{11,10},{12,13},{15,14},{16,17},{19,... | collective-permute-start | bytes 3145736 | tf_op jit(solution)/shard_map/ppermute | solution.py:182
  56.9 1.0 copy-start.2
  57.9 18.9 %copy-start.7 = (f32[1024,256]{1,0:T(8,128)S(1)}, f32[1024,256]{1,0:T(8,128)}, u32[]{:S(2)}) copy-start(f32[1024,256]{1,0:T(8,128)} %get-tuple-element.28) | copy-start | bytes 3145732
  59.1 44.8 %collective-permute-start.1 = (f32[1152,256]{1,0:T(8,128)}, f32[1152,256]{1,0:T(8,128)S(1)}, u32[]{:S(2)}, u32[]{:S(2)}) collective-permute-start(f32[1152,256]{1,0:T(8,128)} %add.124), channel_id=1, source_target_pairs={{1,2},{2,1},{5,6},{6,5},{9,10},{10,9},{13,14},{14,13},{17,18},{18,... | collective-permute-start | bytes 3538952 | tf_op jit(solution)/shard_map/ppermute | solution.py:218
  79.2 33.4 %collective-permute-start.3 = (f32[1024,256]{1,0:T(8,128)}, f32[1024,256]{1,0:T(8,128)}, u32[]{:S(2)}, u32[]{:S(2)}) collective-permute-start(f32[1024,256]{1,0:T(8,128)} %add.126), channel_id=1, source_target_pairs={{1,2},{2,1},{5,6},{6,5},{9,10},{10,9},{13,14},{14,13},{17,18},{18,... | collective-permute-start | bytes 3145736 | tf_op jit(solution)/shard_map/ppermute | solution.py:216
  81.5 45.2 %collective-permute-start.5 = (f32[1024,256]{1,0:T(8,128)}, f32[1024,256]{1,0:T(8,128)}, u32[]{:S(2)}, u32[]{:S(2)}) collective-permute-start(f32[1024,256]{1,0:T(8,128)} %get-tuple-element.32), channel_id=1, source_target_pairs={{0,1},{3,2},{4,5},{7,6},{8,9},{11,10},{12,13},{15,14},{16,17},{19,... | collective-permute-start | bytes 3145736 | tf_op jit(solution)/shard_map/ppermute | solution.py:182
  101.5 33.1 %collective-permute-start.8 = (f32[1024,256]{1,0:T(8,128)}, f32[1024,256]{1,0:T(8,128)}, u32[]{:S(2)}, u32[]{:S(2)}) collective-permute-start(f32[1024,256]{1,0:T(8,128)} %add.130), channel_id=1, source_target_pairs={{1,2},{2,1},{5,6},{6,5},{9,10},{10,9},{13,14},{14,13},{17,18},{18,... | collective-permute-start | bytes 3145736 | tf_op jit(solution)/shard_map/ppermute | solution.py:182
  103.9 11.4 %collective-permute-start.10 = (f32[128,256]{1,0:T(8,128)S(1)}, f32[128,256]{1,0:T(8,128)S(1)}, u32[]{:S(2)}, u32[]{:S(2)}) collective-permute-start(f32[128,256]{1,0:T(8,128)S(1)} %slice_add_fusion.2), channel_id=1, source_target_pairs={{2,3},{1,0},{6,7},{5,4},{10,11},{9,8},{14,15},{13,12},{18,19},{17,... | collective-permute-start | bytes 393224 | tf_op jit(solution)/shard_map/ppermute | solution.py:127
  115.3 31.2 %collective-permute-start.4 = (f32[1024,256]{1,0:T(8,128)}, f32[1024,256]{1,0:T(8,128)}, u32[]{:S(2)}, u32[]{:S(2)}) collective-permute-start(f32[1024,256]{1,0:T(8,128)} %add.127), channel_id=1, source_target_pairs={{0,1},{2,3},{1,0},{3,2},{4,5},{6,7},{5,4},{7,6},{8,9},{10,11},{9,8... | collective-permute-start | bytes 3145736 | tf_op jit(solution)/shard_map/ppermute | solution.py:182
  116.9 10.0 %copy-start.6 = (f32[1024,256]{1,0:T(8,128)S(1)}, f32[1024,256]{1,0:T(8,128)}, u32[]{:S(2)}) copy-start(f32[1024,256]{1,0:T(8,128)} %get-tuple-element.31) | copy-start | bytes 3145732
  122.4 14.7 %collective-permute-start.13 = (f32[2,4096]{1,0:T(2,128)}, f32[2,4096]{1,0:T(2,128)S(1)}, u32[]{:S(2)}, u32[]{:S(2)}) collective-permute-start(f32[2,4096]{1,0:T(2,128)} %reshape.46), channel_id=1, source_target_pairs={{0,3},{1,2},{2,1},{3,0},{4,7},{5,6},{6,5},{7,4},{8,11},{9,10},{10,... | collective-permute-start | bytes 98312 | tf_op jit(solution)/shard_map/ppermute | solution.py:230
  122.8 21.8 %collective-permute-start.12 = (f32[2,4096]{1,0:T(2,128)}, f32[2,4096]{1,0:T(2,128)S(1)}, u32[]{:S(2)}, u32[]{:S(2)}) collective-permute-start(f32[2,4096]{1,0:T(2,128)} %reshape.46), channel_id=1, source_target_pairs={{0,2},{1,3},{2,0},{3,1},{4,6},{5,7},{6,4},{7,5},{8,10},{9,11},{10,... | collective-permute-start | bytes 98312 | tf_op jit(solution)/shard_map/ppermute | solution.py:230
  126.7 18.3 %collective-permute-start.11 = (f32[2,4096]{1,0:T(2,128)}, f32[2,4096]{1,0:T(2,128)S(1)}, u32[]{:S(2)}, u32[]{:S(2)}) collective-permute-start(f32[2,4096]{1,0:T(2,128)} %reshape.46), channel_id=1, source_target_pairs={{0,1},{1,0},{2,3},{3,2},{4,5},{5,4},{6,7},{7,6},{8,9},{9,8},{10,11... | collective-permute-start | bytes 98312 | tf_op jit(solution)/shard_map/ppermute | solution.py:230
  126.8 7.8 %copy-start.5 = (f32[1024,256]{1,0:T(8,128)S(1)}, f32[1024,256]{1,0:T(8,128)}, u32[]{:S(2)}) copy-start(f32[1024,256]{1,0:T(8,128)} %get-tuple-element.34) | copy-start | bytes 3145732
  134.6 13.7 %copy-start.9 = (s32[128]{0:T(128)S(1)}, s32[128]{0:T(128)}, u32[]{:S(2)}) copy-start(s32[128]{0:T(128)} %param.14) | copy-start | bytes 1540
  134.6 18.5 %copy-start.4 = (f32[1024,256]{1,0:T(8,128)S(1)}, f32[1024,256]{1,0:T(8,128)}, u32[]{:S(2)}) copy-start(f32[1024,256]{1,0:T(8,128)} %get-tuple-element.23) | copy-start | bytes 3145732
  146.5 5.1 %collective-permute-start.16 = (f32[2,4096]{1,0:T(2,128)}, f32[2,4096]{1,0:T(2,128)}, u32[]{:S(2)}, u32[]{:S(2)}) collective-permute-start(f32[2,4096]{1,0:T(2,128)} %add_add_fusion), channel_id=1, source_target_pairs={{0,12},{4,8},{8,4},{12,0},{1,13},{5,9},{9,5},{13,1},{2,14},{6,10},... | collective-permute-start | bytes 98312 | tf_op jit(solution)/shard_map/ppermute | solution.py:234
  146.6 4.9 %collective-permute-start.15 = (f32[2,4096]{1,0:T(2,128)}, f32[2,4096]{1,0:T(2,128)}, u32[]{:S(2)}, u32[]{:S(2)}) collective-permute-start(f32[2,4096]{1,0:T(2,128)} %add_add_fusion), channel_id=1, source_target_pairs={{0,8},{4,12},{8,0},{12,4},{1,9},{5,13},{9,1},{13,5},{2,10},{6,14},... | collective-permute-start | bytes 98312 | tf_op jit(solution)/shard_map/ppermute | solution.py:234
  148.0 3.6 %collective-permute-start.14 = (f32[2,4096]{1,0:T(2,128)}, f32[2,4096]{1,0:T(2,128)}, u32[]{:S(2)}, u32[]{:S(2)}) collective-permute-start(f32[2,4096]{1,0:T(2,128)} %add_add_fusion), channel_id=1, source_target_pairs={{0,4},{4,0},{8,12},{12,8},{1,5},{5,1},{9,13},{13,9},{2,6},{6,2},{1... | collective-permute-start | bytes 98312 | tf_op jit(solution)/shard_map/ppermute | solution.py:234
  148.4 27.2 %collective-permute-start.6 = (f32[1024,256]{1,0:T(8,128)S(1)}, f32[1024,256]{1,0:T(8,128)}, u32[]{:S(2)}, u32[]{:S(2)}) collective-permute-start(f32[1024,256]{1,0:T(8,128)S(1)} %add.129), channel_id=1, source_target_pairs={{1,2},{2,1},{5,6},{6,5},{9,10},{10,9},{13,14},{14,13},{17,18},{18,... | collective-permute-start | bytes 3145736 | tf_op jit(solution)/shard_map/ppermute | solution.py:182
  151.5 25.3 %collective-permute-start.9 = (f32[1024,256]{1,0:T(8,128)}, f32[1024,256]{1,0:T(8,128)}, u32[]{:S(2)}, u32[]{:S(2)}) collective-permute-start(f32[1024,256]{1,0:T(8,128)} %add.131), channel_id=1, source_target_pairs={{0,1},{2,3},{1,0},{3,2},{4,5},{6,7},{5,4},{7,6},{8,9},{10,11},{9,8... | collective-permute-start | bytes 3145736 | tf_op jit(solution)/shard_map/ppermute | solution.py:182
  152.4 0.7 copy-start.8
  154.5 22.3 %copy-start.3 = (f32[1024,256]{1,0:T(8,128)S(1)}, f32[1024,256]{1,0:T(8,128)}, u32[]{:S(2)}) copy-start(f32[1024,256]{1,0:T(8,128)} %get-tuple-element.30) | copy-start | bytes 3145732
  161.7 3.1 %collective-permute-start.19 = (f32[2,16]{1,0:T(2,128)S(1)}, f32[2,16]{1,0:T(2,128)S(1)}, u32[]{:S(2)}, u32[]{:S(2)}) collective-permute-start(f32[2,16]{1,0:T(2,128)S(1)} %get-tuple-element.42), channel_id=1, source_target_pairs={{0,12},{4,8},{8,4},{12,0},{1,13},{5,9},{9,5},{13,1},{2,14},{6,10},... | collective-permute-start | bytes 392 | tf_op jit(solution)/shard_map/ppermute | solution.py:243
  162.6 3.6 %collective-permute-start.18 = (f32[2,16]{1,0:T(2,128)S(1)}, f32[2,16]{1,0:T(2,128)S(1)}, u32[]{:S(2)}, u32[]{:S(2)}) collective-permute-start(f32[2,16]{1,0:T(2,128)S(1)} %get-tuple-element.43), channel_id=1, source_target_pairs={{0,8},{4,12},{8,0},{12,4},{1,9},{5,13},{9,1},{13,5},{2,10},{6,14},... | collective-permute-start | bytes 392 | tf_op jit(solution)/shard_map/ppermute | solution.py:243
  163.4 2.8 %collective-permute-start.17 = (f32[2,16]{1,0:T(2,128)S(1)}, f32[2,16]{1,0:T(2,128)S(1)}, u32[]{:S(2)}, u32[]{:S(2)}) collective-permute-start(f32[2,16]{1,0:T(2,128)S(1)} %get-tuple-element.44), channel_id=1, source_target_pairs={{0,4},{4,0},{8,12},{12,8},{1,5},{5,1},{9,13},{13,9},{2,6},{6,2},{1... | collective-permute-start | bytes 392 | tf_op jit(solution)/shard_map/ppermute | solution.py:243

commit v3 on v2

--- a/solution.py
+++ b/solution.py
@@ -19,66 +19,155 @@
     return next(c for c in choices if size % c == 0)
 
 
-def front_kernel(feat, picks, extra, block_ref, tok_ref, w_ref, act_ref, *refs):
-    pieces = [(k, own, feat // split, r) for k, own, split in picks for r in range(split)]
-    grad_ref, part_refs = refs[-1 - len(pieces)], refs[len(refs) - len(pieces):]
-
-    @pl.when(pl.program_id(0) == 0)
-    def _():
-        for part_ref in part_refs:
-            part_ref[...] = jnp.zeros_like(part_ref)
-        if extra:
-            cols_ref, proj_ref = refs[:2]
-            factor = lax.dot_general(
-                proj_ref[...], cols_ref[...], (((1,), (1,)), ((), ())), preferred_element_type=jnp.float32
-            )
-            for d in range(factor.shape[1] // LEN):
-                at = slice(d * factor.shape[0], (d + 1) * factor.shape[0])
-                part_refs[-1][at, :] = factor[:, d * LEN:(d + 1) * LEN]
-
-    preact = jnp.dot(tok_ref[...], w_ref[...], preferred_element_type=jnp.float32)
+def activation_gradient(preact, act):
     sig = 1.0 / (1.0 + jnp.exp(-preact))
     slopes = sig * (1.0 + preact * (1.0 - sig))
-    grad = (act_ref[...].astype(jnp.float32) * slopes).astype(jnp.bfloat16).T
-    grad_ref[...] = grad
-    for part_ref, (k, own, rows, r) in zip(part_refs, pieces):
-        start = pl.multiple_of(block_ref[k] * feat + r * rows, rows)
-        right = grad if own else refs[0][...]
-        part_ref[part_ref.shape[0] - rows:, :] += jnp.dot(w_ref[pl.ds(start, rows), :], right, preferred_element_type=jnp.float32)
-
-
-def front(doc, blocks, picks, tokens, weight, grad_act, other, proj_in, feat, earlier):
+    return (act.astype(jnp.float32) * slopes).astype(jnp.bfloat16)
+
+
+def front_kernel(doc, ahead, picks, lead, n, tok_any, w_any, act_any, extra_any, proj_any, grad_any, *refs):
+    part_refs = refs[:len(picks)]
+    tok, w, act, grad, pre, extra, proj, single, w_sem, out_sem = refs[len(picks):]
+    slices, width, cols = w.shape
+    feat = part_refs[-1].shape[0]
+    pos = lax.axis_index("tensor")
+    rows = pl.ds(doc * LEN, LEN)
+
+    def first_row(k):
+        if lead and n == 4:
+            k = jnp.where((pos > 0) & (pos < n - 1), 3 - k, k)
+        return pl.multiple_of(lax.rem(pos + jnp.where(lax.rem(pos, 2) == 0, n - k, k), n) * feat, feat)
+    tok_copy = pltpu.make_async_copy(tok_any.at[rows, :], tok, single.at[0])
+    act_copy = pltpu.make_async_copy(act_any.at[rows, :], act, single.at[1])
+    if lead:
+        place = pl.multiple_of(pos * feat, feat)
+        extra_copy = pltpu.make_async_copy(extra_any.at[:, pl.ds(place, feat)], extra, single.at[2])
+        proj_copy = pltpu.make_async_copy(proj_any, proj, single.at[3])
+    else:
+        extra_copy = pltpu.make_async_copy(extra_any, extra, single.at[2])
+
+    def w_copy(j):
+        return pltpu.make_async_copy(w_any.at[:, pl.ds(j * cols, cols)], w.at[j], w_sem.at[j])
+
+    def out_copy(j):
+        return pltpu.make_async_copy(grad.at[j], grad_any.at[pl.ds(j * cols, cols), :], out_sem.at[j])
+
+    def preact(j):
+        w_copy(j).wait()
+        return jnp.dot(tok[...], w[j], preferred_element_type=jnp.float32)
+
+    def use(j):
+        at = pl.multiple_of(j * cols, cols)
+        here = activation_gradient(pre[j % 2], act[:, pl.ds(at, cols)]).T
+        grad[j] = here
+        for out_ref, (k, own) in zip(part_refs, picks):
+            right = here if own else extra[pl.ds(at, cols), :]
+            out_ref[out_ref.shape[0] - feat:, :] += jnp.dot(
+                w[j, pl.ds(first_row(k), feat), :], right, preferred_element_type=jnp.float32
+            )
+        out_copy(j).start()
+
+    tok_copy.start()
+    w_copy(0).start()
+    act_copy.start()
+    for j in range(1, ahead):
+        w_copy(j).start()
+    if not lead:
+        extra_copy.start()
+    for out_ref in part_refs:
+        out_ref[...] = jnp.zeros_like(out_ref)
+    tok_copy.wait()
+    pre[0] = preact(0)
+    act_copy.wait()
+    if not lead:
+        extra_copy.wait()
+
+    def step(j, carry):
+        @pl.when(j + ahead - 1 < slices)
+        def _():
+            w_copy(j + ahead - 1).start()
+
+        if lead:
+            @pl.when(j + ahead - 1 == slices)
+            def _():
+                extra_copy.start()
+                proj_copy.start()
+
+        now = preact(j)
+        use(j - 1)
+        pre[j % 2] = now
+        return carry
+
+    lax.fori_loop(1, slices, step, 0)
+    if lead:
+        extra_copy.wait()
+        proj_copy.wait()
+        factor = lax.dot_general(proj[...], extra[...], (((1,), (1,)), ((), ())), preferred_element_type=jnp.float32)
+        for d in range(factor.shape[1] // LEN):
+            part_refs[0][d * factor.shape[0]:(d + 1) * factor.shape[0], :] = factor[:, d * LEN:(d + 1) * LEN]
+    use(slices - 1)
+    for j in range(slices):
+        out_copy(j).wait()
+
+
+def front(doc, n, picks, tokens, weight, grad_act, other, proj_in, feat):
     width, hidden = weight.shape
     cols = widest(hidden, (512, 256, 128))
-    rows = [feat // split for _, _, split in picks for _ in range(split)]
-    more, more_specs = list(other), [pl.BlockSpec((cols, LEN), lambda j, b: (j, 0))] * len(other)
-    if proj_in is not None:
-        more = [tokens, proj_in]
-        more_specs = [
-            pl.BlockSpec((tokens.shape[0], feat), lambda j, b: (0, b[len(picks)])),
-            pl.BlockSpec(proj_in.shape, lambda j, b: (0, 0)),
-        ]
-        rows[-1] += tokens.shape[0] // LEN * proj_in.shape[0]
-    return pl.pallas_call(
-        functools.partial(front_kernel, feat, picks, proj_in is not None),
+    slices = hidden // cols
+    rows = [feat] * len(picks)
+    lead = other is None
+    if lead:
+        rows[0] += tokens.shape[0] // LEN * proj_in.shape[0]
+    return pl.pallas_call(
+        functools.partial(front_kernel, doc, 3, picks, lead, n),
         grid_spec=pltpu.PrefetchScalarGridSpec(
-            num_scalar_prefetch=1,
-            grid=(hidden // cols,),
-            in_specs=[
-                pl.BlockSpec((LEN, width), lambda j, b: (doc, 0)),
-                pl.BlockSpec((width, cols), lambda j, b: (0, j)),
-                pl.BlockSpec((LEN, cols), lambda j, b: (doc, j)),
-            ]
-            + more_specs
-            + [pl.BlockSpec(memory_space=pl.ANY)] * len(earlier),
-            out_specs=[pl.BlockSpec((cols, LEN), lambda j, b: (j, 0))]
-            + [pl.BlockSpec((size, LEN), lambda j, b: (0, 0)) for size in rows],
+            num_scalar_prefetch=0,
+            grid=(1,),
+            in_specs=[pl.BlockSpec(memory_space=pl.ANY)] * 5,
+            out_specs=[pl.BlockSpec(memory_space=pl.ANY)] + [pl.BlockSpec((size, LEN), lambda i: (0, 0)) for size in rows],
+            scratch_shapes=[
+                pltpu.VMEM((LEN, width), jnp.bfloat16),
+                pltpu.VMEM((slices, width, cols), jnp.bfloat16),
+                pltpu.VMEM((LEN, hidden), jnp.bfloat16),
+                pltpu.VMEM((slices, cols, LEN), jnp.bfloat16),
+                pltpu.VMEM((2, LEN, cols), jnp.float32),
+                pltpu.VMEM((tokens.shape[0], feat) if lead else (hidden, LEN), jnp.bfloat16),
+                pltpu.VMEM(proj_in.shape, jnp.bfloat16),
+                pltpu.SemaphoreType.DMA((4,)),
+                pltpu.SemaphoreType.DMA((slices,)),
+                pltpu.SemaphoreType.DMA((slices,)),
+            ],
         ),
         out_shape=[jax.ShapeDtypeStruct((hidden, LEN), jnp.bfloat16)]
         + [jax.ShapeDtypeStruct((size, LEN), jnp.float32) for size in rows],
         compiler_params=pltpu.CompilerParams(vmem_limit_bytes=VMEM),
         cost_estimate=BRIEF,
-    )(blocks, tokens, weight, grad_act, *more, *earlier)
+    )(tokens, weight, grad_act, tokens if lead else other, proj_in)
+
+
+def own_blocks_kernel(block_ref, w_ref, *refs):
+    count = len(refs) // 2
+    for grad_ref, out_ref in zip(refs[:count], refs[count:]):
+        out_ref[...] = jnp.dot(w_ref[...], grad_ref[...], preferred_element_type=jnp.float32)
+
+
+def own_blocks(blocks, weight, grads, feat):
+    hidden = weight.shape[1]
+    tile = min(256, feat)
+    steps = feat // tile
+    return pl.pallas_call(
+        own_blocks_kernel,
+        grid_spec=pltpu.PrefetchScalarGridSpec(
+            num_scalar_prefetch=1,
+            grid=(steps,),
+            in_specs=[pl.BlockSpec((tile, hidden), lambda i, b: (b[0] * steps + i, 0))]
+            + [pl.BlockSpec((hidden, LEN), lambda i, b: (0, 0))] * len(grads),
+            out_specs=[pl.BlockSpec((tile, LEN), lambda i, b: (i, 0))] * len(grads),
+        ),
+        out_shape=[jax.ShapeDtypeStruct((feat, LEN), jnp.float32)] * len(grads),
+        compiler_params=pltpu.CompilerParams(vmem_limit_bytes=VMEM),
+        cost_estimate=BRIEF,
+    )(blocks, weight, *grads)
 
 
 def sketch_kernel(widths, proj_ref, in_ref, *refs):
@@ -153,11 +242,28 @@
     )(mine, everyone, *earlier)
 
 
+def finish_kernel(done_ref, *refs):
+    out_ref, width = refs[-1], done_ref.shape[1]
+    out_ref[:, :width] = done_ref[...]
+    out_ref[:, width:] = functools.reduce(jnp.add, [ref[...] for ref in refs[:-1]]).astype(out_ref.dtype)
+
+
+def finish(done, parts):
+    feat, width = done.shape
+    tile = min(256, feat)
+    return pl.pallas_call(
+        finish_kernel,
+        grid=(feat // tile,),
+        in_specs=[pl.BlockSpec((tile, x.shape[1]), lambda i: (i, 0)) for x in (done, *parts)],
+        out_specs=pl.BlockSpec((tile, width + parts[0].shape[1]), lambda i: (i, 0)),
+        out_shape=jax.ShapeDtypeStruct((feat, width + parts[0].shape[1]), done.dtype),
+        compiler_params=pltpu.CompilerParams(vmem_limit_bytes=16 << 20),
+        cost_estimate=BRIEF,
+    )(done, *parts)
+
+
 def after(x, *others):
     return lax.optimization_barrier((x, *others))[0]
-
-
-SPLITS = (1, 1)
 
 
 class Line:
@@ -194,32 +300,23 @@
     line = Line(n)
     order = (pos + sign * jnp.arange(n, dtype=jnp.int32)) % n
 
-    def make(doc, blocks, picks, other, proj):
-        return front(doc, blocks, picks, tokens, weight, grad_act, other, proj, feat, [])
-
     short = n == 4
-    inner = (pos > 0) & (pos < n - 1) & short
-    held = (pos + sign * (jnp.arange(2, dtype=jnp.int32) + 1 + jnp.where(inner, jnp.array([1, -1], jnp.int32), 0))) % n
-    held = jnp.concatenate([held, pos.astype(jnp.int32).reshape(1)])
-    grad, near, far = make(0, held, [(0, True, 1), (1, True, 1)], [], proj_in.T)
-    size = far.shape[0] - feat
+    grad, near, far = front(0, n, [(1, True), (2, True)], tokens, weight, grad_act, None, proj_in.T, feat)
+    size = near.shape[0] - feat
     near_in, far_in = (lax.ppermute(x, "tensor", line_pairs(n, 1, 0)) for x in (near, far))
-    for k, block, arrived in ((1, near, near_in), (2, far[size:], far_in[size:])):
+    for k, block, arrived in ((1, near[size:], near_in[size:]), (2, far, far_in)):
         line.blocks[k, 0, 0], line.received[k, 0, 0, 0] = block, arrived
-    picks = [(k % n, True, 1) for k in range(1, n + 1)] + [(k % n, False, 1) for k in range(3, n + 1)]
-    other, *parts = make(1, order, picks, [grad], None)
-    for (k, own, _), part in zip(picks, parts):
+    picks = [(k, True) for k in range(1, n)] + [(k, False) for k in range(3, n)]
+    other, *parts = front(1, n, picks, tokens, weight, grad_act, grad, proj_in.T, feat)
+    for (k, own), part in zip(picks, parts):
         line.blocks[k, 1 if own else 0, 0] = part
     grads = [grad, other]
-    factor_in = Total(far[:size], n, [far_in[:size]])
+    factor_in = Total(near[:size], n, [after(near_in, other, far_in)[:size]])
     if short:
-        line.received[2, 1, 0, 0] = lax.ppermute(near + after(near_in, other), "tensor", line_pairs(n, 2, 1))
-        far_sum = far + after(far_in, other)
-        passed = lax.ppermute(far_sum, "tensor", line_pairs(n, 3, 1))
-        line.received[3, 1, 0, 0] = passed[size:]
-        factor_in.hops.append(passed[:size])
-        line.received[1, 0, 1, 0] = after(line.send(1, 0, 1, 0)[0], far_sum)
-        line.received[2, 0, 1, 0] = after(line.send(2, 0, 1, 0)[0], line.sum_of(3, 0, 0, 0))
+        near_sum = near[size:] + after(near_in, other)[size:]
+        line.received[2, 1, 0, 0] = lax.ppermute(near_sum, "tensor", line_pairs(n, 2, 1))
+        factor_in.hop()
+        factor_in.hops[-1] = after(factor_in.hops[-1], line.received[2, 1, 0, 0])
     while len(factor_in.hops) + 1 < n:
         factor_in.hop()
 
@@ -227,12 +324,18 @@
         return after(x, *(line.send(*place)[0] for place in places)) if short else x
 
     sketches = sketch(proj_out.T, factor_in.result(), grads, []).reshape(docs, SK)
+    if short:
+        line.received[1, 0, 1, 0] = after(line.send(1, 0, 1, 0)[0], sketches)
+        far_sum = far + after(far_in, line.sum_of(2, 1, 1, 0))
+        line.received[3, 1, 0, 0] = lax.ppermute(far_sum, "tensor", line_pairs(n, 3, 1))
+        line.received[2, 0, 1, 0] = after(line.send(2, 0, 1, 0)[0], line.sum_of(3, 0, 0, 0))
     others = [lax.ppermute(sketches, "tensor", [(i, i ^ far) for i in range(n)]) for far in range(1, n)]
-    own = gate(functools.reduce(jnp.add, others, sketches), (3, 0, 0, 0))
+    own = functools.reduce(jnp.add, others, sketches)
     if short:
-        own = after(own, line.sum_of(3, 1, 1, 0), line.sum_of(3, 0, 1, 0))
+        own = after(own, line.sum_of(3, 0, 1, 0), line.sum_of(3, 1, 1, 0))
     others = [lax.ppermute(own, "dp", [(i, i ^ far) for i in range(m)]) for far in range(1, m)]
-    everyone = jnp.concatenate([own, *others], 0)
+    line.blocks[0, 0, 0], line.blocks[0, 1, 0] = own_blocks(order, weight, [after(grad, own), other], feat)
+    everyone = gate(after(jnp.concatenate([own, *others], 0), line.blocks[0, 1, 0]), (3, 0, 0, 0), (3, 1, 0, 0))
     gram_rows = SK // (m * n)
     mine = lax.dynamic_slice_in_dim(everyone, (dp_pos * n + pos) * gram_rows, gram_rows, 1)
     gram = gram_rows_of(mine, everyone, [])
@@ -246,19 +349,17 @@
     places = jnp.concatenate([(dp_pos ^ far) * bank + jnp.arange(bank, dtype=query_index.dtype) for far in range(m)])
     for step in range(1, n):
         for doc in range(docs):
-            for r in range(SPLITS[doc]):
+            for r in range(1):
                 line.send(step, 0, doc, r)
                 line.send(step, 1, doc, r)
 
-    outs = [[] for _ in range(docs)]
+    ends = []
     for doc in range(docs):
-        for r in range(SPLITS[doc]):
-            total = line.blocks[0, doc, r]
-            last = [line.received[n - 1, color, doc, r] for color in (1, 0) if (n - 1, color, doc, r) in line.received]
-            for part in lax.optimization_barrier((*last, scores))[:-1] if short and doc == docs - 1 else last:
-                total = total + part
-            outs[doc].append(total.astype(jnp.bfloat16))
-    grad_in_t = jnp.concatenate([jnp.concatenate(row, 0) for row in outs], 1)
+        last = [line.received[n - 1, color, doc, 0] for color in (1, 0) if (n - 1, color, doc, 0) in line.received]
+        if short and doc == docs - 1:
+            last = lax.optimization_barrier((*last, scores))[:-1]
+        ends.append([line.blocks[0, doc, 0], *last])
+    grad_in_t = finish(functools.reduce(jnp.add, ends[0]).astype(jnp.bfloat16), ends[1])
 
     picked = jnp.where(query_index[None, :, None] == places[None, None, :], scores[:, None, :], 0.0)
     return (grad_in_t, gram, jnp.sum(picked, -1))

time: 182 us -> 171 us (0.940); the launches traced: 180 us -> 170 us
  other arithmetic: 23.1 us -> 16.5 us
  waiting for transfers between devices: 65.9 us -> 59.4 us
  Pallas kernels: 60.4 us -> 63.2 us
  starting transfers between devices: 24.7 us -> 27.4 us
    ppermute x6, waiting for transfers between devices: 32.6 us -> 22.2 us  [send(): lax.ppermute(block, 'tensor', line_pairs(self.count, step, color))]
    ppermute x3, waiting for transfers between devices: 8.04 us -> 0.01 us  [body(): lax.ppermute(sketches, 'tensor', [(i, i ^ far) for i in range(n)])]
    ppermute x2, waiting for transfers between devices: 15.4 us -> 21.8 us  [body(): lax.ppermute(x, 'tensor', line_pairs(n, 1, 0))]
    ppermute x1 -> x2, waiting for transfers between devices: 0.01 us -> 5.58 us  [hop(): self.hops.append(lax.ppermute(send, 'tensor', pairs))]
    pallas_call x2 -> x4, Pallas kernels: 50.5 us -> 53.4 us  [the longest x2 42.5 us: front(): pl.pallas_call(functools.partial(front_kernel, doc, 3, picks, lead, n), g...]
    ppermute x1 -> x2, starting transfers between devices: 1.3 us -> 3.82 us  [hop(): self.hops.append(lax.ppermute(send, 'tensor', pairs))]
    concatenate x3 -> x1, other arithmetic: 2.5 us -> 0.07 us  [body(): jnp.concatenate([own, *others], 0)]
    add x3, other arithmetic: 4.92 us -> 2.6 us  [the longest x1 1.45 us: body(): far_sum = far + after(far_in, line.sum_of(2, 1, 1, 0))]
  transfers between devices with their start and end apart: 20 -> 21, of which waited for: 10 -> 11; matrix products, arithmetic and copies ran while one was open for 13% -> 11% of each run, Pallas kernels for 22% -> 25%
where the time goes in v3:
time: 171 us; the launch traced here: 170 us
  Pallas kernels  63.2 us (37%)
  waiting for transfers between devices  59.4 us (35%)
  starting transfers between devices  27.4 us (16%)
  other arithmetic  16.5 us (10%)
    pallas_call x2, Pallas kernels, front(): pl.pallas_call(functools.partial(front_kernel, doc, 3, picks, lead, n), g...  42.5 us
    ppermute x6, waiting for transfers between devices, send(): lax.ppermute(block, 'tensor', line_pairs(self.count, step, color))  22.2 us
    ppermute x2, waiting for transfers between devices, body(): lax.ppermute(x, 'tensor', line_pairs(n, 1, 0))  21.8 us
    add x4, other arithmetic, sum_of(): self.sums[place] = block + before[0] if before else block  9.71 us
    pallas_call x1, Pallas kernels, own_blocks(): pl.pallas_call(own_blocks_kernel, grid_spec=pltpu.PrefetchScalarGridSpec(...  9.28 us
    ppermute x1, waiting for transfers between devices, body(): lax.ppermute(far_sum, 'tensor', line_pairs(n, 3, 1))  7.99 us
    ppermute x6, starting transfers between devices, send(): lax.ppermute(block, 'tensor', line_pairs(self.count, step, color))  7.54 us
    pallas_call x1, Pallas kernels, gram_rows_of(): pl.pallas_call(gram_kernel, grid=(width // cols,), in_specs=[pl.BlockSpec...  5.96 us
  transfers between devices with their start and end apart: 21, of which 11 were waited for; matrix products, arithmetic and copies ran while one was open for 11% of the time, Pallas kernels for 25%

profile of v3, /device:TPU:16, one launch (start us, length us, event | category | flops | bytes accessed | tf_op | source)
XLA Modules:
  0.0 170.4 jit_solution(7754245251088346479)
XLA Ops:
  0.6 0.0 copy-start
  0.6 18.2 %shard_map.94 = (bf16[3584,256]{1,0:T(8,128)(2,1)}, f32[1152,256]{1,0:T(8,128)}, f32[1024,256]{1,0:T(8,128)}) custom-call(bf16[512,4096]{1,0:T(8,128)(2,1)} %tok_any.3, bf16[4096,3584]{1,0:T(8,128)(2,1)} %w_ref.1, bf16[512,3584]{1,0:T(8,128)(2,1)} %act_any.3, bf16[512,4096]{1,0:T(8,128)(2,1)} %tok_any.3, bf16[64,1024]{1,0:T(8,128)(2,1)} %bitcast.4), custom_call_target="tpu_custom_call" | custom-call | flops 1 | bytes 1 | tf_op jit(solution)/shard_map/pallas_call | solution.py:121
  18.8 1.3 collective-permute-start
  20.1 1.3 collective-permute-start.1
  21.5 24.3 %shard_map.95 = (bf16[3584,256]{1,0:T(8,128)(2,1)}, f32[1024,256]{1,0:T(8,128)}, f32[1024,256]{1,0:T(8,128)}, f32[1024,256]{1,0:T(8,128)}, f32[1024,256]{1,0:T(8,128)}) custom-call(bf16[512,4096]{1,0:T(8,128)(2,1)} %tok_any.3, bf16[4096,3584]{1,0:T(8,128)(2,1)} %w_ref.1, bf16[512,3584]{1,0:T(8,128)(2,1)} %act_any.3, ...), custom_call_target="tpu_custom_call" | custom-call | flops 1 | bytes 1 | tf_op jit(solution)/shard_map/pallas_call | solution.py:121
  45.8 4.0 %collective-permute-done = f32[1152,256]{1,0:T(8,128)S(1)} collective-permute-done((f32[1152,256]{1,0:T(8,128)}, f32[1152,256]{1,0:T(8,128)S(1)}, u32[]{:S(2)}, u32[]{:S(2)}) %collective-permute-start) | collective-permute-done | bytes 1179680 | tf_op jit(solution)/shard_map/ppermute | solution.py:306
  49.8 1.1 slice_add_fusion
  50.9 2.3 %collective-permute-start.3 = (f32[1024,256]{1,0:T(8,128)}, f32[1024,256]{1,0:T(8,128)}, u32[]{:S(2)}, u32[]{:S(2)}) collective-permute-start(f32[1024,256]{1,0:T(8,128)} %slice_add_fusion), channel_id=1, source_target_pairs={{1,2},{2,1},{5,6},{6,5},{9,10},{10,9},{13,14},{14,13},{17,18},{18,... | collective-permute-start | bytes 3145736 | tf_op jit(solution)/shard_map/ppermute | solution.py:317
  53.3 1.3 collective-permute-start.8
  54.6 17.8 %collective-permute-done.1 = f32[1024,256]{1,0:T(8,128)} collective-permute-done((f32[1024,256]{1,0:T(8,128)}, f32[1024,256]{1,0:T(8,128)}, u32[]{:S(2)}, u32[]{:S(2)}) %collective-permute-start.1) | collective-permute-done | bytes 1048608 | tf_op jit(solution)/shard_map/ppermute | solution.py:306
  72.4 2.4 %collective-permute-start.2 = (f32[128,256]{1,0:T(8,128)S(1)}, f32[128,256]{1,0:T(8,128)S(1)}, u32[]{:S(2)}, u32[]{:S(2)}) collective-permute-start(f32[128,256]{1,0:T(8,128)S(1)} %slice_add_fusion.1), channel_id=1, source_target_pairs={{1,2},{2,1},{5,6},{6,5},{9,10},{10,9},{13,14},{14,13},{17,18},{18,... | collective-permute-start | bytes 393224 | tf_op jit(solution)/shard_map/ppermute | solution.py:216
  74.8 1.3 collective-permute-start.10
  76.1 3.2 %collective-permute-done.2 = f32[128,256]{1,0:T(8,128)S(1)} collective-permute-done((f32[128,256]{1,0:T(8,128)S(1)}, f32[128,256]{1,0:T(8,128)S(1)}, u32[]{:S(2)}, u32[]{:S(2)}) %collective-permute-start.2) | collective-permute-done | bytes 131104 | tf_op jit(solution)/shard_map/ppermute | solution.py:216
  79.3 0.0 collective-permute-done.3
  79.3 1.5 collective-permute-start.4
  80.8 0.1 pad_add_fusion
  80.9 2.4 %collective-permute-done.4 = f32[128,256]{1,0:T(8,128)S(1)} collective-permute-done((f32[128,256]{1,0:T(8,128)S(1)}, f32[128,256]{1,0:T(8,128)S(1)}, u32[]{:S(2)}, u32[]{:S(2)}) %collective-permute-start.4) | collective-permute-done | bytes 131104 | tf_op jit(solution)/shard_map/ppermute | solution.py:216
  83.3 0.7 add_add_fusion.in_ref
  83.9 3.9 %shard_map.96 = f32[2,64,64]{2,1,0:T(8,128)} custom-call(bf16[64,3584]{1,0:T(8,128)(2,1)} %bitcast.6, f32[128,256]{1,0:T(8,128)} %add_add_fusion.in_ref, bf16[3584,256]{1,0:T(8,128)(2,1)} %get-tuple-element.40.extra_any.refs_0_, bf16[3584,256]{1,0:T(8,128)(2,1)} %get-tuple-element.28.refs_1_), custom_call_target="tpu_custom_call" | custom-call | flops 1 | bytes 1 | tf_op jit(solution)/shard_map/pallas_call | solution.py:191
  87.8 0.9 reshape.42
  88.7 0.0 copy-start.7
  88.8 1.6 collective-permute-start.7
  90.4 3.2 %collective-permute-start.6 = (f32[2,4096]{1,0:T(2,128)S(1)}, f32[2,4096]{1,0:T(2,128)S(1)}, u32[]{:S(2)}, u32[]{:S(2)}) collective-permute-start(f32[2,4096]{1,0:T(2,128)S(1)} %reshape.42), channel_id=1, source_target_pairs={{0,2},{1,3},{2,0},{3,1},{4,6},{5,7},{6,4},{7,5},{8,10},{9,11},{10,... | collective-permute-start | bytes 98312 | tf_op jit(solution)/shard_map/ppermute | solution.py:332
  93.6 0.1 collective-permute-start.5
  93.8 1.1 collective-permute-done.8
  94.9 2.7 %add.104 = f32[1024,256]{1,0:T(8,128)} add(f32[1024,256]{1,0:T(8,128)} %get-tuple-element.34, f32[1024,256]{1,0:T(8,128)} %collective-permute-done.8) | non-fusion elementwise | flops 262144 | bytes 3145728 | tf_op jit(solution)/shard_map/add | solution.py:281
  97.5 2.3 %collective-permute-start.9 = (f32[1024,256]{1,0:T(8,128)}, f32[1024,256]{1,0:T(8,128)}, u32[]{:S(2)}, u32[]{:S(2)}) collective-permute-start(f32[1024,256]{1,0:T(8,128)} %add.104), channel_id=1, source_target_pairs={{1,2},{2,1},{5,6},{6,5},{9,10},{10,9},{13,14},{14,13},{17,18},{18,... | collective-permute-start | bytes 3145736 | tf_op jit(solution)/shard_map/ppermute | solution.py:288
  99.9 0.1 broadcast_compare_fusion
  100.0 2.4 %add.106 = f32[1024,256]{1,0:T(8,128)} add(f32[1024,256]{1,0:T(8,128)S(1)} %copy-done.6, f32[1024,256]{1,0:T(8,128)} %collective-permute-done.3) | non-fusion elementwise | flops 262144 | bytes 3145728 | tf_op jit(solution)/shard_map/add | solution.py:281
  102.3 14.8 %collective-permute-done.10 = f32[1024,256]{1,0:T(8,128)S(1)} collective-permute-done((f32[1024,256]{1,0:T(8,128)}, f32[1024,256]{1,0:T(8,128)S(1)}, u32[]{:S(2)}, u32[]{:S(2)}) %collective-permute-start.10) | collective-permute-done | bytes 1048608 | tf_op jit(solution)/shard_map/ppermute | solution.py:288
  117.1 0.0 collective-permute-start.12
  117.1 2.4 %add.107 = f32[1024,256]{1,0:T(8,128)} add(f32[1024,256]{1,0:T(8,128)} %get-tuple-element.35, f32[1024,256]{1,0:T(8,128)S(1)} %collective-permute-done.10) | non-fusion elementwise | flops 262144 | bytes 3145728 | tf_op jit(solution)/shard_map/add | solution.py:281
  119.5 1.4 add.108
  121.0 0.0 collective-permute-done.7
  121.0 2.4 %collective-permute-start.11 = (f32[1024,256]{1,0:T(8,128)S(1)}, f32[1024,256]{1,0:T(8,128)}, u32[]{:S(2)}, u32[]{:S(2)}) collective-permute-start(f32[1024,256]{1,0:T(8,128)S(1)} %add.108), channel_id=1, source_target_pairs={{1,2},{2,1},{5,6},{6,5},{9,10},{10,9},{13,14},{14,13},{17,18},{18,... | collective-permute-start | bytes 3145736 | tf_op jit(solution)/shard_map/ppermute | solution.py:330
  123.3 0.0 collective-permute-done.6
  123.3 0.0 collective-permute-done.5
  123.4 1.0 collective-permute-done.9
  124.3 2.3 %add.105 = f32[1024,256]{1,0:T(8,128)} add(f32[1024,256]{1,0:T(8,128)S(1)} %copy-done.4, f32[1024,256]{1,0:T(8,128)} %collective-permute-done.9) | non-fusion elementwise | flops 262144 | bytes 3145728 | tf_op jit(solution)/shard_map/add | solution.py:281
  126.7 0.0 collective-permute-start.17
  126.7 1.5 collective-permute-start.16
  128.2 0.3 collective-permute-start.15
  128.5 0.5 and_select_fusion.block_ref
  129.1 9.3 %shard_map.97 = (f32[1024,256]{1,0:T(8,128)}, f32[1024,256]{1,0:T(8,128)}) custom-call(s32[4]{0:T(128)} %and_select_fusion.block_ref, bf16[4096,3584]{1,0:T(8,128)(2,1)} %w_ref.1, bf16[3584,256]{1,0:T(8,128)(2,1)} %get-tuple-element.40.extra_any.refs_0_, bf16[3584,256]{1,0:T(8,128)(2,1)} %get-tuple-element.28.refs_1_), custom_call_target="tpu_custom_call" | custom-call | flops 1 | bytes 1 | tf_op jit(solution)/shard_map/pallas_call | solution.py:158
  138.3 0.0 collective-permute-done.17
  138.3 2.5 %collective-permute-start.13 = (f32[1024,256]{1,0:T(8,128)}, f32[1024,256]{1,0:T(8,128)S(1)}, u32[]{:S(2)}, u32[]{:S(2)}) collective-permute-start(f32[1024,256]{1,0:T(8,128)} %add.107), channel_id=1, source_target_pairs={{1,2},{2,1},{5,6},{6,5},{9,10},{10,9},{13,14},{14,13},{17,18},{18,... | collective-permute-start | bytes 3145736 | tf_op jit(solution)/shard_map/ppermute | solution.py:288
  140.9 0.1 collective-permute-start.14
  141.0 0.1 pad_maximum_fusion.all_ref
  141.1 0.0 collective-permute-done.12
  141.1 8.0 %collective-permute-done.11 = f32[1024,256]{1,0:T(8,128)} collective-permute-done((f32[1024,256]{1,0:T(8,128)S(1)}, f32[1024,256]{1,0:T(8,128)}, u32[]{:S(2)}, u32[]{:S(2)}) %collective-permute-start.11) | collective-permute-done | bytes 1048608 | tf_op jit(solution)/shard_map/ppermute | solution.py:330
  149.1 0.6 constant_dynamic-slice_fusion.mine_ref
  149.7 2.0 %add_convert_fusion.done_ref = bf16[1024,256]{1,0:T(8,128)(2,1)S(1)} fusion(f32[1024,256]{1,0:T(8,128)} %collective-permute-done.12, f32[1024,256]{1,0:T(8,128)} %get-tuple-element.41, f32[1024,256]{1,0:T(8,128)} %collective-permute-done.11), kind=kLoop, calls=%fused_computation.1 | loop fusion | flops 786432 | bytes 3670016 | tf_op jit(solution)/shard_map/convert_element_type | solution.py:362
  151.7 6.0 %shard_map.98 = f32[256,4096]{1,0:T(8,128)} custom-call(f32[8,256]{1,0:T(8,128)} %constant_dynamic-slice_fusion.mine_ref, f32[8,4096]{1,0:T(8,128)} %copy-done.3), custom_call_target="tpu_custom_call" | custom-call | flops 1 | bytes 1 | tf_op jit(solution)/shard_map/pallas_call | solution.py:233
  157.7 1.3 convolution_multiply_fusion
  159.0 0.1 collective-permute-start.20
  159.1 1.6 collective-permute-start.19
  160.6 0.3 collective-permute-start.18
  160.9 1.1 collective-permute-done.20
  162.0 0.7 collective-permute-done.19
  162.7 0.0 collective-permute-done.18
  162.7 0.1 pad_maximum_fusion.1
  162.8 0.7 select_reduce_fusion
  163.4 5.4 %collective-permute-done.13.refs_1_ = f32[1024,256]{1,0:T(8,128)S(1)} collective-permute-done((f32[1024,256]{1,0:T(8,128)}, f32[1024,256]{1,0:T(8,128)S(1)}, u32[]{:S(2)}, u32[]{:S(2)}) %collective-permute-start.13) | collective-permute-done | bytes 1048608 | tf_op jit(solution)/shard_map/ppermute | solution.py:288
  168.8 1.6 shard_map.99
  (23 shorter events, 0.1 us)
Async XLA Ops:
  0.6 157.0 %copy-start = (f32[16,4096]{1,0:T(8,128)S(1)}, f32[16,4096]{1,0:T(8,128)}, u32[]{:S(2)}) copy-start(f32[16,4096]{1,0:T(8,128)} %param.12) | copy-start | bytes 786436
  18.8 31.0 %collective-permute-start = (f32[1152,256]{1,0:T(8,128)}, f32[1152,256]{1,0:T(8,128)S(1)}, u32[]{:S(2)}, u32[]{:S(2)}) collective-permute-start(f32[1152,256]{1,0:T(8,128)} %get-tuple-element.27), channel_id=1, source_target_pairs={{0,1},{3,2},{4,5},{7,6},{8,9},{11,10},{12,13},{15,14},{16,17},{19,... | collective-permute-start | bytes 3538952 | tf_op jit(solution)/shard_map/ppermute | solution.py:306
  20.1 52.2 %collective-permute-start.1 = (f32[1024,256]{1,0:T(8,128)}, f32[1024,256]{1,0:T(8,128)}, u32[]{:S(2)}, u32[]{:S(2)}) collective-permute-start(f32[1024,256]{1,0:T(8,128)} %get-tuple-element.29), channel_id=1, source_target_pairs={{0,1},{3,2},{4,5},{7,6},{8,9},{11,10},{12,13},{15,14},{16,17},{19,... | collective-permute-start | bytes 3145736 | tf_op jit(solution)/shard_map/ppermute | solution.py:306
  21.4 28.4 %copy-start.2 = (f32[1152,256]{1,0:T(8,128)S(1)}, f32[1152,256]{1,0:T(8,128)}, u32[]{:S(2)}) copy-start(f32[1152,256]{1,0:T(8,128)} %get-tuple-element.27) | copy-start | bytes 3538948
  50.9 28.3 %collective-permute-start.3 = (f32[1024,256]{1,0:T(8,128)}, f32[1024,256]{1,0:T(8,128)}, u32[]{:S(2)}, u32[]{:S(2)}) collective-permute-start(f32[1024,256]{1,0:T(8,128)} %slice_add_fusion), channel_id=1, source_target_pairs={{1,2},{2,1},{5,6},{6,5},{9,10},{10,9},{13,14},{14,13},{17,18},{18,... | collective-permute-start | bytes 3145736 | tf_op jit(solution)/shard_map/ppermute | solution.py:317
  53.3 41.6 %collective-permute-start.8 = (f32[1024,256]{1,0:T(8,128)}, f32[1024,256]{1,0:T(8,128)}, u32[]{:S(2)}, u32[]{:S(2)}) collective-permute-start(f32[1024,256]{1,0:T(8,128)} %get-tuple-element.35), channel_id=1, source_target_pairs={{0,1},{3,2},{4,5},{7,6},{8,9},{11,10},{12,13},{15,14},{16,17},{19,... | collective-permute-start | bytes 3145736 | tf_op jit(solution)/shard_map/ppermute | solution.py:288
  72.4 6.9 %collective-permute-start.2 = (f32[128,256]{1,0:T(8,128)S(1)}, f32[128,256]{1,0:T(8,128)S(1)}, u32[]{:S(2)}, u32[]{:S(2)}) collective-permute-start(f32[128,256]{1,0:T(8,128)S(1)} %slice_add_fusion.1), channel_id=1, source_target_pairs={{1,2},{2,1},{5,6},{6,5},{9,10},{10,9},{13,14},{14,13},{17,18},{18,... | collective-permute-start | bytes 393224 | tf_op jit(solution)/shard_map/ppermute | solution.py:216
  74.8 42.4 %collective-permute-start.10 = (f32[1024,256]{1,0:T(8,128)}, f32[1024,256]{1,0:T(8,128)S(1)}, u32[]{:S(2)}, u32[]{:S(2)}) collective-permute-start(f32[1024,256]{1,0:T(8,128)} %get-tuple-element.34), channel_id=1, source_target_pairs={{0,1},{3,2},{4,5},{7,6},{8,9},{11,10},{12,13},{15,14},{16,17},{19,... | collective-permute-start | bytes 3145736 | tf_op jit(solution)/shard_map/ppermute | solution.py:288
  79.3 4.0 %collective-permute-start.4 = (f32[128,256]{1,0:T(8,128)S(1)}, f32[128,256]{1,0:T(8,128)S(1)}, u32[]{:S(2)}, u32[]{:S(2)}) collective-permute-start(f32[128,256]{1,0:T(8,128)S(1)} %slice_add_fusion.2), channel_id=1, source_target_pairs={{2,3},{1,0},{6,7},{5,4},{10,11},{9,8},{14,15},{13,12},{18,19},{17,... | collective-permute-start | bytes 393224 | tf_op jit(solution)/shard_map/ppermute | solution.py:216
  88.7 11.1 %copy-start.7 = (s32[128]{0:T(128)S(1)}, s32[128]{0:T(128)}, u32[]{:S(2)}) copy-start(s32[128]{0:T(128)} %param.13) | copy-start | bytes 1540
  88.8 11.2 %copy-start.6 = (f32[1024,256]{1,0:T(8,128)S(1)}, f32[1024,256]{1,0:T(8,128)}, u32[]{:S(2)}) copy-start(f32[1024,256]{1,0:T(8,128)} %get-tuple-element.37) | copy-start | bytes 3145732
  88.8 32.2 %collective-permute-start.7 = (f32[2,4096]{1,0:T(2,128)S(1)}, f32[2,4096]{1,0:T(2,128)S(1)}, u32[]{:S(2)}, u32[]{:S(2)}) collective-permute-start(f32[2,4096]{1,0:T(2,128)S(1)} %reshape.42), channel_id=1, source_target_pairs={{0,3},{1,2},{2,1},{3,0},{4,7},{5,6},{6,5},{7,4},{8,11},{9,10},{10,... | collective-permute-start | bytes 98312 | tf_op jit(solution)/shard_map/ppermute | solution.py:332
  90.4 32.9 %collective-permute-start.6 = (f32[2,4096]{1,0:T(2,128)S(1)}, f32[2,4096]{1,0:T(2,128)S(1)}, u32[]{:S(2)}, u32[]{:S(2)}) collective-permute-start(f32[2,4096]{1,0:T(2,128)S(1)} %reshape.42), channel_id=1, source_target_pairs={{0,2},{1,3},{2,0},{3,1},{4,6},{5,7},{6,4},{7,5},{8,10},{9,11},{10,... | collective-permute-start | bytes 98312 | tf_op jit(solution)/shard_map/ppermute | solution.py:332
  93.6 29.7 %collective-permute-start.5 = (f32[2,4096]{1,0:T(2,128)S(1)}, f32[2,4096]{1,0:T(2,128)S(1)}, u32[]{:S(2)}, u32[]{:S(2)}) collective-permute-start(f32[2,4096]{1,0:T(2,128)S(1)} %reshape.42), channel_id=1, source_target_pairs={{0,1},{1,0},{2,3},{3,2},{4,5},{5,4},{6,7},{7,6},{8,9},{9,8},{10,11... | collective-permute-start | bytes 98312 | tf_op jit(solution)/shard_map/ppermute | solution.py:332
  97.5 26.8 %collective-permute-start.9 = (f32[1024,256]{1,0:T(8,128)}, f32[1024,256]{1,0:T(8,128)}, u32[]{:S(2)}, u32[]{:S(2)}) collective-permute-start(f32[1024,256]{1,0:T(8,128)} %add.104), channel_id=1, source_target_pairs={{1,2},{2,1},{5,6},{6,5},{9,10},{10,9},{13,14},{14,13},{17,18},{18,... | collective-permute-start | bytes 3145736 | tf_op jit(solution)/shard_map/ppermute | solution.py:288
  102.3 17.2 %copy-start.5 = (f32[1024,256]{1,0:T(8,128)S(1)}, f32[1024,256]{1,0:T(8,128)}, u32[]{:S(2)}) copy-start(f32[1024,256]{1,0:T(8,128)} %get-tuple-element.29) | copy-start | bytes 3145732
  117.1 23.9 %collective-permute-start.12 = (f32[1024,256]{1,0:T(8,128)}, f32[1024,256]{1,0:T(8,128)}, u32[]{:S(2)}, u32[]{:S(2)}) collective-permute-start(f32[1024,256]{1,0:T(8,128)} %add.106), channel_id=1, source_target_pairs={{0,1},{2,3},{1,0},{3,2},{4,5},{6,7},{5,4},{7,6},{8,9},{10,11},{9,8... | collective-permute-start | bytes 3145736 | tf_op jit(solution)/shard_map/ppermute | solution.py:288
  119.5 4.8 %copy-start.4 = (f32[1024,256]{1,0:T(8,128)S(1)}, f32[1024,256]{1,0:T(8,128)}, u32[]{:S(2)}) copy-start(f32[1024,256]{1,0:T(8,128)} %get-tuple-element.33) | copy-start | bytes 3145732
  121.0 28.1 %collective-permute-start.11 = (f32[1024,256]{1,0:T(8,128)S(1)}, f32[1024,256]{1,0:T(8,128)}, u32[]{:S(2)}, u32[]{:S(2)}) collective-permute-start(f32[1024,256]{1,0:T(8,128)S(1)} %add.108), channel_id=1, source_target_pairs={{1,2},{2,1},{5,6},{6,5},{9,10},{10,9},{13,14},{14,13},{17,18},{18,... | collective-permute-start | bytes 3145736 | tf_op jit(solution)/shard_map/ppermute | solution.py:330
  126.7 11.7 %collective-permute-start.17 = (f32[2,4096]{1,0:T(2,128)S(1)}, f32[2,4096]{1,0:T(2,128)S(1)}, u32[]{:S(2)}, u32[]{:S(2)}) collective-permute-start(f32[2,4096]{1,0:T(2,128)S(1)} %add_add_fusion.1), channel_id=1, source_target_pairs={{0,12},{4,8},{8,4},{12,0},{1,13},{5,9},{9,5},{13,1},{2,14},{6,10},... | collective-permute-start | bytes 98312 | tf_op jit(solution)/shard_map/ppermute | solution.py:336
  126.7 14.2 %collective-permute-start.16 = (f32[2,4096]{1,0:T(2,128)S(1)}, f32[2,4096]{1,0:T(2,128)S(1)}, u32[]{:S(2)}, u32[]{:S(2)}) collective-permute-start(f32[2,4096]{1,0:T(2,128)S(1)} %add_add_fusion.1), channel_id=1, source_target_pairs={{0,8},{4,12},{8,0},{12,4},{1,9},{5,13},{9,1},{13,5},{2,10},{6,14},... | collective-permute-start | bytes 98312 | tf_op jit(solution)/shard_map/ppermute | solution.py:336
  128.2 12.8 %collective-permute-start.15 = (f32[2,4096]{1,0:T(2,128)S(1)}, f32[2,4096]{1,0:T(2,128)S(1)}, u32[]{:S(2)}, u32[]{:S(2)}) collective-permute-start(f32[2,4096]{1,0:T(2,128)S(1)} %add_add_fusion.1), channel_id=1, source_target_pairs={{0,4},{4,0},{8,12},{12,8},{1,5},{5,1},{9,13},{13,9},{2,6},{6,2},{1... | collective-permute-start | bytes 98312 | tf_op jit(solution)/shard_map/ppermute | solution.py:336
  138.3 30.5 %collective-permute-start.13 = (f32[1024,256]{1,0:T(8,128)}, f32[1024,256]{1,0:T(8,128)S(1)}, u32[]{:S(2)}, u32[]{:S(2)}) collective-permute-start(f32[1024,256]{1,0:T(8,128)} %add.107), channel_id=1, source_target_pairs={{1,2},{2,1},{5,6},{6,5},{9,10},{10,9},{13,14},{14,13},{17,18},{18,... | collective-permute-start | bytes 3145736 | tf_op jit(solution)/shard_map/ppermute | solution.py:288
  140.9 27.9 %collective-permute-start.14 = (f32[1024,256]{1,0:T(8,128)}, f32[1024,256]{1,0:T(8,128)S(1)}, u32[]{:S(2)}, u32[]{:S(2)}) collective-permute-start(f32[1024,256]{1,0:T(8,128)} %add.105), channel_id=1, source_target_pairs={{0,1},{2,3},{1,0},{3,2},{4,5},{6,7},{5,4},{7,6},{8,9},{10,11},{9,8... | collective-permute-start | bytes 3145736 | tf_op jit(solution)/shard_map/ppermute | solution.py:288
  141.1 10.6 %copy-start.3 = (f32[8,4096]{1,0:T(8,128)}, f32[8,4096]{1,0:T(8,128)S(1)}, u32[]{:S(2)}) copy-start(f32[8,4096]{1,0:T(8,128)S(1)} %pad_maximum_fusion.all_ref) | copy-start | bytes 393220
  151.7 17.1 %copy-start.1 = (f32[1024,256]{1,0:T(8,128)S(1)}, f32[1024,256]{1,0:T(8,128)}, u32[]{:S(2)}) copy-start(f32[1024,256]{1,0:T(8,128)} %get-tuple-element.43.refs_0_) | copy-start | bytes 3145732
  159.0 3.1 %collective-permute-start.20 = (f32[2,16]{1,0:T(2,128)S(1)}, f32[2,16]{1,0:T(2,128)S(1)}, u32[]{:S(2)}, u32[]{:S(2)}) collective-permute-start(f32[2,16]{1,0:T(2,128)S(1)} %get-tuple-element.50), channel_id=1, source_target_pairs={{0,12},{4,8},{8,4},{12,0},{1,13},{5,9},{9,5},{13,1},{2,14},{6,10},... | collective-permute-start | bytes 392 | tf_op jit(solution)/shard_map/ppermute | solution.py:346
  159.1 3.6 %collective-permute-start.19 = (f32[2,16]{1,0:T(2,128)S(1)}, f32[2,16]{1,0:T(2,128)S(1)}, u32[]{:S(2)}, u32[]{:S(2)}) collective-permute-start(f32[2,16]{1,0:T(2,128)S(1)} %get-tuple-element.51), channel_id=1, source_target_pairs={{0,8},{4,12},{8,0},{12,4},{1,9},{5,13},{9,1},{13,5},{2,10},{6,14},... | collective-permute-start | bytes 392 | tf_op jit(solution)/shard_map/ppermute | solution.py:346
  160.6 2.1 %collective-permute-start.18 = (f32[2,16]{1,0:T(2,128)S(1)}, f32[2,16]{1,0:T(2,128)S(1)}, u32[]{:S(2)}, u32[]{:S(2)}) collective-permute-start(f32[2,16]{1,0:T(2,128)S(1)} %get-tuple-element.52), channel_id=1, source_target_pairs={{0,4},{4,0},{8,12},{12,8},{1,5},{5,1},{9,13},{13,9},{2,6},{6,2},{1... | collective-permute-start | bytes 392 | tf_op jit(solution)/shard_map/ppermute | solution.py:346

commit v4 on v3

--- a/solution.py
+++ b/solution.py
@@ -328,13 +328,17 @@
         line.received[1, 0, 1, 0] = after(line.send(1, 0, 1, 0)[0], sketches)
         far_sum = far + after(far_in, line.sum_of(2, 1, 1, 0))
         line.received[3, 1, 0, 0] = lax.ppermute(far_sum, "tensor", line_pairs(n, 3, 1))
-        line.received[2, 0, 1, 0] = after(line.send(2, 0, 1, 0)[0], line.sum_of(3, 0, 0, 0))
+        held = [after(grad, line.sum_of(2, 1, 1, 0)), other]
+        line.blocks[0, 0, 0], line.blocks[0, 1, 0] = own_blocks(order, weight, held, feat)
+        ready = (line.sum_of(3, 0, 0, 0), line.blocks[0, 1, 0])
+        line.received[2, 0, 1, 0] = after(line.send(2, 0, 1, 0)[0], *ready)
     others = [lax.ppermute(sketches, "tensor", [(i, i ^ far) for i in range(n)]) for far in range(1, n)]
     own = functools.reduce(jnp.add, others, sketches)
     if short:
         own = after(own, line.sum_of(3, 0, 1, 0), line.sum_of(3, 1, 1, 0))
     others = [lax.ppermute(own, "dp", [(i, i ^ far) for i in range(m)]) for far in range(1, m)]
-    line.blocks[0, 0, 0], line.blocks[0, 1, 0] = own_blocks(order, weight, [after(grad, own), other], feat)
+    if not short:
+        line.blocks[0, 0, 0], line.blocks[0, 1, 0] = own_blocks(order, weight, grads, feat)
     everyone = gate(after(jnp.concatenate([own, *others], 0), line.blocks[0, 1, 0]), (3, 0, 0, 0), (3, 1, 0, 0))
     gram_rows = SK // (m * n)
     mine = lax.dynamic_slice_in_dim(everyone, (dp_pos * n + pos) * gram_rows, gram_rows, 1)

time: 171 us -> 172 us (level)
  waiting for transfers between devices: 59.4 us -> 62.1 us
    ppermute x6, waiting for transfers between devices: 22.2 us -> 25.2 us  [send(): lax.ppermute(block, 'tensor', line_pairs(self.count, step, color))]
    add x4, other arithmetic: 9.71 us -> 7.6 us  [sum_of(): self.sums[place] = block + before[0] if before else block]
  transfers between devices with their start and end apart: 21 -> 21, of which waited for: 11 -> 11; matrix products, arithmetic and copies ran while one was open for 11% -> 10% of each run, Pallas kernels for 25% -> 25%
where the time goes in v4:
time: 172 us; the launch traced here: 171 us
  Pallas kernels  63.2 us (37%)
  waiting for transfers between devices  62.1 us (36%)
  starting transfers between devices  26.9 us (16%)
  other arithmetic  15.1 us (9%)
    pallas_call x2, Pallas kernels, front(): pl.pallas_call(functools.partial(front_kernel, doc, 3, picks, lead, n), g...  42.5 us
    ppermute x6, waiting for transfers between devices, send(): lax.ppermute(block, 'tensor', line_pairs(self.count, step, color))  25.2 us
    ppermute x2, waiting for transfers between devices, body(): lax.ppermute(x, 'tensor', line_pairs(n, 1, 0))  21.9 us
    pallas_call x1, Pallas kernels, own_blocks(): pl.pallas_call(own_blocks_kernel, grid_spec=pltpu.PrefetchScalarGridSpec(...  9.3 us
    ppermute x6, starting transfers between devices, send(): lax.ppermute(block, 'tensor', line_pairs(self.count, step, color))  8.5 us
    add x4, other arithmetic, sum_of(): self.sums[place] = block + before[0] if before else block  7.6 us
    ppermute x1, waiting for transfers between devices, body(): lax.ppermute(far_sum, 'tensor', line_pairs(n, 3, 1))  6.73 us
    pallas_call x1, Pallas kernels, gram_rows_of(): pl.pallas_call(gram_kernel, grid=(width // cols,), in_specs=[pl.BlockSpec...  5.97 us
  transfers between devices with their start and end apart: 21, of which 11 were waited for; matrix products, arithmetic and copies ran while one was open for 10% of the time, Pallas kernels for 25%

profile of v4, /device:TPU:16, one launch (start us, length us, event | category | flops | bytes accessed | tf_op | source)
XLA Modules:
  0.0 171.1 jit_solution(6796810288033342073)
XLA Ops:
  0.6 0.0 copy-start
  0.6 18.2 %shard_map.94 = (bf16[3584,256]{1,0:T(8,128)(2,1)}, f32[1152,256]{1,0:T(8,128)}, f32[1024,256]{1,0:T(8,128)}) custom-call(bf16[512,4096]{1,0:T(8,128)(2,1)} %tok_any.3, bf16[4096,3584]{1,0:T(8,128)(2,1)} %w_ref.1, bf16[512,3584]{1,0:T(8,128)(2,1)} %act_any.3, bf16[512,4096]{1,0:T(8,128)(2,1)} %tok_any.3, bf16[64,1024]{1,0:T(8,128)(2,1)} %bitcast.4), custom_call_target="tpu_custom_call" | custom-call | flops 1 | bytes 1 | tf_op jit(solution)/shard_map/pallas_call | solution.py:121
  18.8 1.3 collective-permute-start.1
  20.1 1.3 collective-permute-start.2
  21.5 24.3 %shard_map.95 = (bf16[3584,256]{1,0:T(8,128)(2,1)}, f32[1024,256]{1,0:T(8,128)}, f32[1024,256]{1,0:T(8,128)}, f32[1024,256]{1,0:T(8,128)}, f32[1024,256]{1,0:T(8,128)}) custom-call(bf16[512,4096]{1,0:T(8,128)(2,1)} %tok_any.3, bf16[4096,3584]{1,0:T(8,128)(2,1)} %w_ref.1, bf16[512,3584]{1,0:T(8,128)(2,1)} %act_any.3, ...), custom_call_target="tpu_custom_call" | custom-call | flops 1 | bytes 1 | tf_op jit(solution)/shard_map/pallas_call | solution.py:121
  45.8 4.0 %collective-permute-done.1 = f32[1152,256]{1,0:T(8,128)S(1)} collective-permute-done((f32[1152,256]{1,0:T(8,128)}, f32[1152,256]{1,0:T(8,128)S(1)}, u32[]{:S(2)}, u32[]{:S(2)}) %collective-permute-start.1) | collective-permute-done | bytes 1179680 | tf_op jit(solution)/shard_map/ppermute | solution.py:306
  49.8 1.1 slice_add_fusion
  50.9 2.3 %collective-permute-start.4 = (f32[1024,256]{1,0:T(8,128)}, f32[1024,256]{1,0:T(8,128)}, u32[]{:S(2)}, u32[]{:S(2)}) collective-permute-start(f32[1024,256]{1,0:T(8,128)} %slice_add_fusion), channel_id=1, source_target_pairs={{1,2},{2,1},{5,6},{6,5},{9,10},{10,9},{13,14},{14,13},{17,18},{18,... | collective-permute-start | bytes 3145736 | tf_op jit(solution)/shard_map/ppermute | solution.py:317
  53.3 1.3 collective-permute-start
  54.6 17.8 %collective-permute-done.2 = f32[1024,256]{1,0:T(8,128)} collective-permute-done((f32[1024,256]{1,0:T(8,128)}, f32[1024,256]{1,0:T(8,128)}, u32[]{:S(2)}, u32[]{:S(2)}) %collective-permute-start.2) | collective-permute-done | bytes 1048608 | tf_op jit(solution)/shard_map/ppermute | solution.py:306
  72.4 2.4 %collective-permute-start.3 = (f32[128,256]{1,0:T(8,128)S(1)}, f32[128,256]{1,0:T(8,128)S(1)}, u32[]{:S(2)}, u32[]{:S(2)}) collective-permute-start(f32[128,256]{1,0:T(8,128)S(1)} %slice_add_fusion.1), channel_id=1, source_target_pairs={{1,2},{2,1},{5,6},{6,5},{9,10},{10,9},{13,14},{14,13},{17,18},{18,... | collective-permute-start | bytes 393224 | tf_op jit(solution)/shard_map/ppermute | solution.py:216
  74.8 1.3 collective-permute-start.8
  76.1 3.2 %collective-permute-done.3 = f32[128,256]{1,0:T(8,128)S(1)} collective-permute-done((f32[128,256]{1,0:T(8,128)S(1)}, f32[128,256]{1,0:T(8,128)S(1)}, u32[]{:S(2)}, u32[]{:S(2)}) %collective-permute-start.3) | collective-permute-done | bytes 131104 | tf_op jit(solution)/shard_map/ppermute | solution.py:216
  79.3 0.0 collective-permute-done.4
  79.3 1.4 collective-permute-start.5
  80.8 2.5 %collective-permute-done.5 = f32[128,256]{1,0:T(8,128)S(1)} collective-permute-done((f32[128,256]{1,0:T(8,128)S(1)}, f32[128,256]{1,0:T(8,128)S(1)}, u32[]{:S(2)}, u32[]{:S(2)}) %collective-permute-start.5) | collective-permute-done | bytes 131104 | tf_op jit(solution)/shard_map/ppermute | solution.py:216
  83.2 0.7 add_add_fusion.in_ref
  83.9 3.9 %shard_map.96 = f32[2,64,64]{2,1,0:T(8,128)} custom-call(bf16[64,3584]{1,0:T(8,128)(2,1)} %bitcast.6, f32[128,256]{1,0:T(8,128)} %add_add_fusion.in_ref, bf16[3584,256]{1,0:T(8,128)(2,1)} %get-tuple-element.36.extra_any.refs_0_, bf16[3584,256]{1,0:T(8,128)(2,1)} %get-tuple-element.30.refs_1_), custom_call_target="tpu_custom_call" | custom-call | flops 1 | bytes 1 | tf_op jit(solution)/shard_map/pallas_call | solution.py:191
  87.8 0.9 reshape.42
  88.7 6.1 %collective-permute-done = f32[1024,256]{1,0:T(8,128)} collective-permute-done((f32[1024,256]{1,0:T(8,128)}, f32[1024,256]{1,0:T(8,128)}, u32[]{:S(2)}, u32[]{:S(2)}) %collective-permute-start) | collective-permute-done | bytes 1048608 | tf_op jit(solution)/shard_map/ppermute | solution.py:288
  94.9 1.7 add.101
  96.5 2.4 %collective-permute-start.10 = (f32[1024,256]{1,0:T(8,128)S(1)}, f32[1024,256]{1,0:T(8,128)S(1)}, u32[]{:S(2)}, u32[]{:S(2)}) collective-permute-start(f32[1024,256]{1,0:T(8,128)S(1)} %add.101), channel_id=1, source_target_pairs={{1,2},{2,1},{5,6},{6,5},{9,10},{10,9},{13,14},{14,13},{17,18},{18,... | collective-permute-start | bytes 3145736 | tf_op jit(solution)/shard_map/ppermute | solution.py:288
  98.9 0.5 and_select_fusion.block_ref
  99.4 0.0 collective-permute-start.12
  99.4 3.0 %collective-permute-start.13 = (f32[2,4096]{1,0:T(2,128)S(1)}, f32[2,4096]{1,0:T(2,128)S(1)}, u32[]{:S(2)}, u32[]{:S(2)}) collective-permute-start(f32[2,4096]{1,0:T(2,128)S(1)} %reshape.42), channel_id=1, source_target_pairs={{0,2},{1,3},{2,0},{3,1},{4,6},{5,7},{6,4},{7,5},{8,10},{9,11},{10,... | collective-permute-start | bytes 98312 | tf_op jit(solution)/shard_map/ppermute | solution.py:335
  102.5 0.4 collective-permute-start.14
  102.9 0.1 pad_add_fusion
  103.0 2.4 %add.104 = f32[1024,256]{1,0:T(8,128)} add(f32[1024,256]{1,0:T(8,128)S(1)} %copy-done.6, f32[1024,256]{1,0:T(8,128)} %collective-permute-done.4) | non-fusion elementwise | flops 262144 | bytes 3145728 | tf_op jit(solution)/shard_map/add | solution.py:281
  105.4 9.3 %shard_map.97 = (f32[1024,256]{1,0:T(8,128)}, f32[1024,256]{1,0:T(8,128)}) custom-call(s32[4]{0:T(128)} %and_select_fusion.block_ref, bf16[4096,3584]{1,0:T(8,128)(2,1)} %w_ref.1, bf16[3584,256]{1,0:T(8,128)(2,1)} %get-tuple-element.36.extra_any.refs_0_, bf16[3584,256]{1,0:T(8,128)(2,1)} %get-tuple-element.30.refs_1_), custom_call_target="tpu_custom_call" | custom-call | flops 1 | bytes 1 | tf_op jit(solution)/shard_map/pallas_call | solution.py:158
  114.7 2.4 %collective-permute-done.8 = f32[1024,256]{1,0:T(8,128)S(1)} collective-permute-done((f32[1024,256]{1,0:T(8,128)}, f32[1024,256]{1,0:T(8,128)S(1)}, u32[]{:S(2)}, u32[]{:S(2)}) %collective-permute-start.8) | collective-permute-done | bytes 1048608 | tf_op jit(solution)/shard_map/ppermute | solution.py:288
  117.1 0.0 collective-permute-start.7
  117.1 2.4 %add.106 = f32[1024,256]{1,0:T(8,128)} add(f32[1024,256]{1,0:T(8,128)} %get-tuple-element.28, f32[1024,256]{1,0:T(8,128)S(1)} %collective-permute-done.8) | non-fusion elementwise | flops 262144 | bytes 3145728 | tf_op jit(solution)/shard_map/add | solution.py:281
  119.6 2.4 %add.102 = f32[1024,256]{1,0:T(8,128)} add(f32[1024,256]{1,0:T(8,128)S(1)} %copy-done.5, f32[1024,256]{1,0:T(8,128)} %collective-permute-done.2) | non-fusion elementwise | flops 262144 | bytes 3145728 | tf_op jit(solution)/shard_map/add | solution.py:329
  122.0 0.0 collective-permute-done.12
  122.0 2.3 %collective-permute-start.6 = (f32[1024,256]{1,0:T(8,128)}, f32[1024,256]{1,0:T(8,128)}, u32[]{:S(2)}, u32[]{:S(2)}) collective-permute-start(f32[1024,256]{1,0:T(8,128)} %add.102), channel_id=1, source_target_pairs={{1,2},{2,1},{5,6},{6,5},{9,10},{10,9},{13,14},{14,13},{17,18},{18,... | collective-permute-start | bytes 3145736 | tf_op jit(solution)/shard_map/ppermute | solution.py:330
  124.3 0.0 collective-permute-done.13
  124.3 0.0 collective-permute-done.14
  124.4 0.0 collective-permute-done.10
  124.4 0.0 copy-start.8
  124.4 1.1 add.107
  125.5 1.5 collective-permute-start.16
  127.0 0.4 collective-permute-start.17
  127.4 0.1 broadcast_compare_fusion
  127.5 0.0 collective-permute-done.15
  127.5 3.5 %collective-permute-start.9 = (f32[1024,256]{1,0:T(8,128)}, f32[1024,256]{1,0:T(8,128)S(1)}, u32[]{:S(2)}, u32[]{:S(2)}) collective-permute-start(f32[1024,256]{1,0:T(8,128)} %add.106), channel_id=1, source_target_pairs={{1,2},{2,1},{5,6},{6,5},{9,10},{10,9},{13,14},{14,13},{17,18},{18,... | collective-permute-start | bytes 3145736 | tf_op jit(solution)/shard_map/ppermute | solution.py:288
  131.0 0.0 collective-permute-done.16
  131.0 0.1 collective-permute-start.11
  131.1 0.1 pad_maximum_fusion.all_ref
  131.2 12.4 %collective-permute-done.7 = f32[1024,256]{1,0:T(8,128)} collective-permute-done((f32[1024,256]{1,0:T(8,128)}, f32[1024,256]{1,0:T(8,128)}, u32[]{:S(2)}, u32[]{:S(2)}) %collective-permute-start.7) | collective-permute-done | bytes 1048608 | tf_op jit(solution)/shard_map/ppermute | solution.py:288
  143.5 6.7 %collective-permute-done.6 = f32[1024,256]{1,0:T(8,128)} collective-permute-done((f32[1024,256]{1,0:T(8,128)}, f32[1024,256]{1,0:T(8,128)}, u32[]{:S(2)}, u32[]{:S(2)}) %collective-permute-start.6) | collective-permute-done | bytes 1048608 | tf_op jit(solution)/shard_map/ppermute | solution.py:330
  150.3 0.6 constant_dynamic-slice_fusion.mine_ref
  150.9 1.7 add_convert_fusion.done_ref
  152.6 6.0 %shard_map.98 = f32[256,4096]{1,0:T(8,128)} custom-call(f32[8,256]{1,0:T(8,128)} %constant_dynamic-slice_fusion.mine_ref, f32[8,4096]{1,0:T(8,128)} %copy-done.3), custom_call_target="tpu_custom_call" | custom-call | flops 1 | bytes 1 | tf_op jit(solution)/shard_map/pallas_call | solution.py:233
  158.6 1.3 convolution_multiply_fusion
  159.9 0.1 collective-permute-start.18
  160.0 1.6 collective-permute-start.19
  161.5 0.3 collective-permute-start.20
  161.8 0.0 collective-permute-done.18
  161.8 1.8 %collective-permute-done.19 = f32[2,16]{1,0:T(2,128)S(1)} collective-permute-done((f32[2,16]{1,0:T(2,128)S(1)}, f32[2,16]{1,0:T(2,128)S(1)}, u32[]{:S(2)}, u32[]{:S(2)}) %collective-permute-start.19) | collective-permute-done | bytes 160 | tf_op jit(solution)/shard_map/ppermute | solution.py:350
  163.6 0.9 collective-permute-done.20
  164.5 0.1 pad_maximum_fusion.1
  164.6 0.7 select_reduce_fusion
  165.3 4.2 %collective-permute-done.9.refs_1_ = f32[1024,256]{1,0:T(8,128)S(1)} collective-permute-done((f32[1024,256]{1,0:T(8,128)}, f32[1024,256]{1,0:T(8,128)S(1)}, u32[]{:S(2)}, u32[]{:S(2)}) %collective-permute-start.9) | collective-permute-done | bytes 1048608 | tf_op jit(solution)/shard_map/ppermute | solution.py:288
  169.5 1.6 shard_map.99
  (25 shorter events, 0.1 us)
Async XLA Ops:
  0.6 157.9 %copy-start = (f32[16,4096]{1,0:T(8,128)S(1)}, f32[16,4096]{1,0:T(8,128)}, u32[]{:S(2)}) copy-start(f32[16,4096]{1,0:T(8,128)} %param.12) | copy-start | bytes 786436
  18.8 31.0 %collective-permute-start.1 = (f32[1152,256]{1,0:T(8,128)}, f32[1152,256]{1,0:T(8,128)S(1)}, u32[]{:S(2)}, u32[]{:S(2)}) collective-permute-start(f32[1152,256]{1,0:T(8,128)} %get-tuple-element.29), channel_id=1, source_target_pairs={{0,1},{3,2},{4,5},{7,6},{8,9},{11,10},{12,13},{15,14},{16,17},{19,... | collective-permute-start | bytes 3538952 | tf_op jit(solution)/shard_map/ppermute | solution.py:306
  20.1 52.2 %collective-permute-start.2 = (f32[1024,256]{1,0:T(8,128)}, f32[1024,256]{1,0:T(8,128)}, u32[]{:S(2)}, u32[]{:S(2)}) collective-permute-start(f32[1024,256]{1,0:T(8,128)} %get-tuple-element.31), channel_id=1, source_target_pairs={{0,1},{3,2},{4,5},{7,6},{8,9},{11,10},{12,13},{15,14},{16,17},{19,... | collective-permute-start | bytes 3145736 | tf_op jit(solution)/shard_map/ppermute | solution.py:306
  21.4 28.4 %copy-start.2 = (f32[1152,256]{1,0:T(8,128)S(1)}, f32[1152,256]{1,0:T(8,128)}, u32[]{:S(2)}) copy-start(f32[1152,256]{1,0:T(8,128)} %get-tuple-element.29) | copy-start | bytes 3538948
  50.9 28.3 %collective-permute-start.4 = (f32[1024,256]{1,0:T(8,128)}, f32[1024,256]{1,0:T(8,128)}, u32[]{:S(2)}, u32[]{:S(2)}) collective-permute-start(f32[1024,256]{1,0:T(8,128)} %slice_add_fusion), channel_id=1, source_target_pairs={{1,2},{2,1},{5,6},{6,5},{9,10},{10,9},{13,14},{14,13},{17,18},{18,... | collective-permute-start | bytes 3145736 | tf_op jit(solution)/shard_map/ppermute | solution.py:317
  53.3 41.6 %collective-permute-start = (f32[1024,256]{1,0:T(8,128)}, f32[1024,256]{1,0:T(8,128)}, u32[]{:S(2)}, u32[]{:S(2)}) collective-permute-start(f32[1024,256]{1,0:T(8,128)} %get-tuple-element.28), channel_id=1, source_target_pairs={{0,1},{3,2},{4,5},{7,6},{8,9},{11,10},{12,13},{15,14},{16,17},{19,... | collective-permute-start | bytes 3145736 | tf_op jit(solution)/shard_map/ppermute | solution.py:288
  72.4 6.9 %collective-permute-start.3 = (f32[128,256]{1,0:T(8,128)S(1)}, f32[128,256]{1,0:T(8,128)S(1)}, u32[]{:S(2)}, u32[]{:S(2)}) collective-permute-start(f32[128,256]{1,0:T(8,128)S(1)} %slice_add_fusion.1), channel_id=1, source_target_pairs={{1,2},{2,1},{5,6},{6,5},{9,10},{10,9},{13,14},{14,13},{17,18},{18,... | collective-permute-start | bytes 393224 | tf_op jit(solution)/shard_map/ppermute | solution.py:216
  74.8 42.4 %collective-permute-start.8 = (f32[1024,256]{1,0:T(8,128)}, f32[1024,256]{1,0:T(8,128)S(1)}, u32[]{:S(2)}, u32[]{:S(2)}) collective-permute-start(f32[1024,256]{1,0:T(8,128)} %get-tuple-element.27), channel_id=1, source_target_pairs={{0,1},{3,2},{4,5},{7,6},{8,9},{11,10},{12,13},{15,14},{16,17},{19,... | collective-permute-start | bytes 3145736 | tf_op jit(solution)/shard_map/ppermute | solution.py:288
  79.3 4.0 %collective-permute-start.5 = (f32[128,256]{1,0:T(8,128)S(1)}, f32[128,256]{1,0:T(8,128)S(1)}, u32[]{:S(2)}, u32[]{:S(2)}) collective-permute-start(f32[128,256]{1,0:T(8,128)S(1)} %slice_add_fusion.2), channel_id=1, source_target_pairs={{2,3},{1,0},{6,7},{5,4},{10,11},{9,8},{14,15},{13,12},{18,19},{17,... | collective-permute-start | bytes 393224 | tf_op jit(solution)/shard_map/ppermute | solution.py:216
  88.7 14.3 %copy-start.6 = (f32[1024,256]{1,0:T(8,128)S(1)}, f32[1024,256]{1,0:T(8,128)}, u32[]{:S(2)}) copy-start(f32[1024,256]{1,0:T(8,128)} %get-tuple-element.39) | copy-start | bytes 3145732
  96.5 27.9 %collective-permute-start.10 = (f32[1024,256]{1,0:T(8,128)S(1)}, f32[1024,256]{1,0:T(8,128)S(1)}, u32[]{:S(2)}, u32[]{:S(2)}) collective-permute-start(f32[1024,256]{1,0:T(8,128)S(1)} %add.101), channel_id=1, source_target_pairs={{1,2},{2,1},{5,6},{6,5},{9,10},{10,9},{13,14},{14,13},{17,18},{18,... | collective-permute-start | bytes 3145736 | tf_op jit(solution)/shard_map/ppermute | solution.py:288
  99.4 22.5 %collective-permute-start.12 = (f32[2,4096]{1,0:T(2,128)S(1)}, f32[2,4096]{1,0:T(2,128)S(1)}, u32[]{:S(2)}, u32[]{:S(2)}) collective-permute-start(f32[2,4096]{1,0:T(2,128)S(1)} %reshape.42), channel_id=1, source_target_pairs={{0,1},{1,0},{2,3},{3,2},{4,5},{5,4},{6,7},{7,6},{8,9},{9,8},{10,11... | collective-permute-start | bytes 98312 | tf_op jit(solution)/shard_map/ppermute | solution.py:335
  99.4 24.9 %collective-permute-start.13 = (f32[2,4096]{1,0:T(2,128)S(1)}, f32[2,4096]{1,0:T(2,128)S(1)}, u32[]{:S(2)}, u32[]{:S(2)}) collective-permute-start(f32[2,4096]{1,0:T(2,128)S(1)} %reshape.42), channel_id=1, source_target_pairs={{0,2},{1,3},{2,0},{3,1},{4,6},{5,7},{6,4},{7,5},{8,10},{9,11},{10,... | collective-permute-start | bytes 98312 | tf_op jit(solution)/shard_map/ppermute | solution.py:335
  102.5 21.9 %collective-permute-start.14 = (f32[2,4096]{1,0:T(2,128)S(1)}, f32[2,4096]{1,0:T(2,128)S(1)}, u32[]{:S(2)}, u32[]{:S(2)}) collective-permute-start(f32[2,4096]{1,0:T(2,128)S(1)} %reshape.42), channel_id=1, source_target_pairs={{0,3},{1,2},{2,1},{3,0},{4,7},{5,6},{6,5},{7,4},{8,11},{9,10},{10,... | collective-permute-start | bytes 98312 | tf_op jit(solution)/shard_map/ppermute | solution.py:335
  117.1 26.4 %collective-permute-start.7 = (f32[1024,256]{1,0:T(8,128)}, f32[1024,256]{1,0:T(8,128)}, u32[]{:S(2)}, u32[]{:S(2)}) collective-permute-start(f32[1024,256]{1,0:T(8,128)} %add.104), channel_id=1, source_target_pairs={{0,1},{2,3},{1,0},{3,2},{4,5},{6,7},{5,4},{7,6},{8,9},{10,11},{9,8... | collective-permute-start | bytes 3145736 | tf_op jit(solution)/shard_map/ppermute | solution.py:288
  117.1 2.4 %copy-start.5 = (f32[1024,256]{1,0:T(8,128)S(1)}, f32[1024,256]{1,0:T(8,128)}, u32[]{:S(2)}) copy-start(f32[1024,256]{1,0:T(8,128)} %get-tuple-element.31) | copy-start | bytes 3145732
  119.6 4.9 %copy-start.4 = (f32[1024,256]{1,0:T(8,128)S(1)}, f32[1024,256]{1,0:T(8,128)}, u32[]{:S(2)}) copy-start(f32[1024,256]{1,0:T(8,128)} %get-tuple-element.42) | copy-start | bytes 3145732
  122.0 28.3 %collective-permute-start.6 = (f32[1024,256]{1,0:T(8,128)}, f32[1024,256]{1,0:T(8,128)}, u32[]{:S(2)}, u32[]{:S(2)}) collective-permute-start(f32[1024,256]{1,0:T(8,128)} %add.102), channel_id=1, source_target_pairs={{1,2},{2,1},{5,6},{6,5},{9,10},{10,9},{13,14},{14,13},{17,18},{18,... | collective-permute-start | bytes 3145736 | tf_op jit(solution)/shard_map/ppermute | solution.py:330
  124.4 3.0 %copy-start.8 = (s32[128]{0:T(128)S(1)}, s32[128]{0:T(128)}, u32[]{:S(2)}) copy-start(s32[128]{0:T(128)} %param.13) | copy-start | bytes 1540
  124.4 26.4 %copy-start.7 = (f32[1024,256]{1,0:T(8,128)S(1)}, f32[1024,256]{1,0:T(8,128)}, u32[]{:S(2)}) copy-start(f32[1024,256]{1,0:T(8,128)} %get-tuple-element.37) | copy-start | bytes 3145732
  125.5 1.9 %collective-permute-start.15 = (f32[2,4096]{1,0:T(2,128)S(1)}, f32[2,4096]{1,0:T(2,128)S(1)}, u32[]{:S(2)}, u32[]{:S(2)}) collective-permute-start(f32[2,4096]{1,0:T(2,128)S(1)} %add_add_fusion.1), channel_id=1, source_target_pairs={{0,4},{4,0},{8,12},{12,8},{1,5},{5,1},{9,13},{13,9},{2,6},{6,2},{1... | collective-permute-start | bytes 98312 | tf_op jit(solution)/shard_map/ppermute | solution.py:339
  125.5 5.4 %collective-permute-start.16 = (f32[2,4096]{1,0:T(2,128)S(1)}, f32[2,4096]{1,0:T(2,128)S(1)}, u32[]{:S(2)}, u32[]{:S(2)}) collective-permute-start(f32[2,4096]{1,0:T(2,128)S(1)} %add_add_fusion.1), channel_id=1, source_target_pairs={{0,8},{4,12},{8,0},{12,4},{1,9},{5,13},{9,1},{13,5},{2,10},{6,14},... | collective-permute-start | bytes 98312 | tf_op jit(solution)/shard_map/ppermute | solution.py:339
  127.0 4.0 %collective-permute-start.17 = (f32[2,4096]{1,0:T(2,128)S(1)}, f32[2,4096]{1,0:T(2,128)S(1)}, u32[]{:S(2)}, u32[]{:S(2)}) collective-permute-start(f32[2,4096]{1,0:T(2,128)S(1)} %add_add_fusion.1), channel_id=1, source_target_pairs={{0,12},{4,8},{8,4},{12,0},{1,13},{5,9},{9,5},{13,1},{2,14},{6,10},... | collective-permute-start | bytes 98312 | tf_op jit(solution)/shard_map/ppermute | solution.py:339
  127.5 42.0 %collective-permute-start.9 = (f32[1024,256]{1,0:T(8,128)}, f32[1024,256]{1,0:T(8,128)S(1)}, u32[]{:S(2)}, u32[]{:S(2)}) collective-permute-start(f32[1024,256]{1,0:T(8,128)} %add.106), channel_id=1, source_target_pairs={{1,2},{2,1},{5,6},{6,5},{9,10},{10,9},{13,14},{14,13},{17,18},{18,... | collective-permute-start | bytes 3145736 | tf_op jit(solution)/shard_map/ppermute | solution.py:288
  131.0 38.5 %collective-permute-start.11 = (f32[1024,256]{1,0:T(8,128)}, f32[1024,256]{1,0:T(8,128)S(1)}, u32[]{:S(2)}, u32[]{:S(2)}) collective-permute-start(f32[1024,256]{1,0:T(8,128)} %add.107), channel_id=1, source_target_pairs={{0,1},{2,3},{1,0},{3,2},{4,5},{6,7},{5,4},{7,6},{8,9},{10,11},{9,8... | collective-permute-start | bytes 3145736 | tf_op jit(solution)/shard_map/ppermute | solution.py:288
  131.2 21.4 %copy-start.3 = (f32[8,4096]{1,0:T(8,128)}, f32[8,4096]{1,0:T(8,128)S(1)}, u32[]{:S(2)}) copy-start(f32[8,4096]{1,0:T(8,128)S(1)} %pad_maximum_fusion.all_ref) | copy-start | bytes 393220
  152.6 16.9 %copy-start.1 = (f32[1024,256]{1,0:T(8,128)S(1)}, f32[1024,256]{1,0:T(8,128)}, u32[]{:S(2)}) copy-start(f32[1024,256]{1,0:T(8,128)} %get-tuple-element.40.refs_0_) | copy-start | bytes 3145732
  159.9 1.9 %collective-permute-start.18 = (f32[2,16]{1,0:T(2,128)S(1)}, f32[2,16]{1,0:T(2,128)S(1)}, u32[]{:S(2)}, u32[]{:S(2)}) collective-permute-start(f32[2,16]{1,0:T(2,128)S(1)} %get-tuple-element.52), channel_id=1, source_target_pairs={{0,4},{4,0},{8,12},{12,8},{1,5},{5,1},{9,13},{13,9},{2,6},{6,2},{1... | collective-permute-start | bytes 392 | tf_op jit(solution)/shard_map/ppermute | solution.py:350
  160.0 3.6 %collective-permute-start.19 = (f32[2,16]{1,0:T(2,128)S(1)}, f32[2,16]{1,0:T(2,128)S(1)}, u32[]{:S(2)}, u32[]{:S(2)}) collective-permute-start(f32[2,16]{1,0:T(2,128)S(1)} %get-tuple-element.51), channel_id=1, source_target_pairs={{0,8},{4,12},{8,0},{12,4},{1,9},{5,13},{9,1},{13,5},{2,10},{6,14},... | collective-permute-start | bytes 392 | tf_op jit(solution)/shard_map/ppermute | solution.py:350
  161.5 3.0 %collective-permute-start.20 = (f32[2,16]{1,0:T(2,128)S(1)}, f32[2,16]{1,0:T(2,128)S(1)}, u32[]{:S(2)}, u32[]{:S(2)}) collective-permute-start(f32[2,16]{1,0:T(2,128)S(1)} %get-tuple-element.50), channel_id=1, source_target_pairs={{0,12},{4,8},{8,4},{12,0},{1,13},{5,9},{9,5},{13,1},{2,14},{6,10},... | collective-permute-start | bytes 392 | tf_op jit(solution)/shard_map/ppermute | solution.py:350
